TPU v7x, 256 devices: a whole 4x4x8 slice. The times are simulated.
256 devices in a mesh: dp: 8 (over y, core), seq: 32 (over z, x).
Axes of the slice: x: 4, y: 4, z: 8, core: 2. Of those that a mesh axis runs over, the one named last changes fastest.
Arguments:
- query: bfloat16 [8, 32, 128, 6144], P('dp', 'seq'), may hold values from -48 to 48
- keys: bfloat16 [8, 32, 128, 6144], P('dp', 'seq'), may hold values from -48 to 48
- values: bfloat16 [8, 32, 128, 6144], P('dp', 'seq'), may hold values from -6 to 6
- grad_out: bfloat16 [8, 32, 128, 6144], P('dp', 'seq'), may hold values from -6 to 6
- frames: int32 [8], replicated, may hold values from 8 to 32, as said below
- bias: float32 [24, 63], replicated, may hold values from -2 to 2
Outputs:
- grad_query: bfloat16 [8, 32, 128, 6144], P('dp', 'seq')
- grad_keys: bfloat16 [8, 32, 128, 6144], P('dp', 'seq')
- grad_values: bfloat16 [8, 32, 128, 6144], P('dp', 'seq')
- bias_grad: float32 [24, 63], replicated
Inputs may be any that keep to these rules, and one draw needn't show every extreme that they name: Some clip has 32 frames.
All inputs are finite; a program needn't handle non-finite values.
Results may differ from a plain program's by a relative error of at most 0.023.
Values may be sent and summed in bfloat16 or wider, within the bound.
No kernel may reach another device: no remote copies, remote signals or barrier semaphores. Data moves between devices by JAX's collectives and lax.ppermute only.
A program may use at most 64 MiB of HBM per device.

v0:
```python
import jax
import jax.numpy as jnp
from jax import lax
from jax.sharding import PartitionSpec as P

SHEADS = 24
THEADS = 24
HDIM = 128


NEG = -1e30


def attend_grads(query, keys, values, grad_out, extra, allowed):
    wide = jnp.float32
    scale_factor = query.shape[-1] ** (-0.5)
    logits = (
        jnp.einsum("bqhd,bkhd->bhqk", query, keys, preferred_element_type=wide) * scale_factor
        + extra
    )
    logits = jnp.where(allowed, logits, NEG)
    row_max = jnp.max(logits, axis=-1, keepdims=True)
    exponent = jnp.exp(logits - row_max)
    attention = exponent / jnp.sum(exponent, axis=-1, keepdims=True)
    attention_low = attention.astype(jnp.bfloat16)
    output = jnp.einsum("bhqk,bkhd->bqhd", attention_low, values, preferred_element_type=wide)
    row_delta = jnp.einsum("bqhd,bqhd->bhq", grad_out, output, preferred_element_type=wide)
    grad_attention = jnp.einsum("bqhd,bkhd->bhqk", grad_out, values, preferred_element_type=wide)
    grad_logits = attention * (grad_attention - row_delta[..., None])
    grad_low = grad_logits.astype(jnp.bfloat16)
    grad_query = (
        jnp.einsum("bhqk,bkhd->bqhd", grad_low, keys, preferred_element_type=wide) * scale_factor
    )
    grad_keys = (
        jnp.einsum("bhqk,bqhd->bkhd", grad_low, query, preferred_element_type=wide) * scale_factor
    )
    grad_values = jnp.einsum(
        "bhqk,bqhd->bkhd", attention_low, grad_out, preferred_element_type=wide
    )
    return (
        grad_query.astype(jnp.bfloat16),
        grad_keys.astype(jnp.bfloat16),
        grad_values.astype(jnp.bfloat16),
        grad_logits,
    )


def offset_table(frame_count):
    positions = jnp.arange(frame_count)
    offsets = positions[None, :] - positions[:, None] + frame_count - 1
    return (offsets[:, :, None] == jnp.arange(2 * frame_count - 1)[None, None, :]).astype(
        jnp.float32
    )


def local(query, keys, values, grad_out, frames, bias):
    frame_count = lax.axis_size("seq")
    frame_index = lax.axis_index("seq")
    length = lax.dynamic_index_in_dim(frames, lax.axis_index("dp"), 0, keepdims=False)
    live_flag = frame_index < length
    patches = query.shape[2]
    split_cols = SHEADS * HDIM
    temporal_cols = THEADS * HDIM
    onehot = offset_table(frame_count)
    bias_table = jnp.einsum("hj,qkj->hqk", bias, onehot, precision=lax.Precision.HIGHEST)
    frame_live = jnp.arange(frame_count) < length
    own_query = query[0, 0]
    own_keys = keys[0, 0]
    own_values = values[0, 0]
    own_grad = grad_out[0, 0] * live_flag.astype(jnp.bfloat16)
    shaped = [
        tensor[:, :split_cols].reshape(1, patches, SHEADS, HDIM)
        for tensor in (own_query, own_keys, own_values, own_grad)
    ]
    grads = attend_grads(shaped[0], shaped[1], shaped[2], shaped[3], 0.0, True)
    spatial = tuple((grad.reshape(patches, split_cols) for grad in grads[:3]))

    def to_rows(tensor):
        return tensor[:, split_cols:].reshape(1, frame_count, patches // frame_count, temporal_cols)

    rows_query = to_rows(own_query)
    rows_keys = to_rows(own_keys)
    rows_values = to_rows(own_values)
    rows_grad = to_rows(own_grad)
    pieces = (
        lax.all_to_all(rows_query, "seq", split_axis=1, concat_axis=0, tiled=True),
        lax.all_to_all(rows_keys, "seq", split_axis=1, concat_axis=0, tiled=True),
        lax.all_to_all(rows_values, "seq", split_axis=1, concat_axis=0, tiled=True),
        lax.all_to_all(rows_grad, "seq", split_axis=1, concat_axis=0, tiled=True),
    )
    item_count = pieces[0].shape[2]

    def arrange(tensor):
        return jnp.transpose(tensor.reshape(frame_count, item_count, THEADS, HDIM), (1, 0, 2, 3))

    def restore(tensor):
        return jnp.transpose(tensor, (1, 0, 2, 3)).reshape(
            frame_count, 1, item_count, temporal_cols
        )

    grads = attend_grads(
        arrange(pieces[0]),
        arrange(pieces[1]),
        arrange(pieces[2]),
        arrange(pieces[3]),
        bias_table[None],
        frame_live,
    )
    bias_part = jnp.einsum("phqk,qkj->hpj", grads[3], onehot, precision=lax.Precision.HIGHEST)
    returned = (
        lax.all_to_all(restore(grads[0]), "seq", split_axis=0, concat_axis=1, tiled=True),
        lax.all_to_all(restore(grads[1]), "seq", split_axis=0, concat_axis=1, tiled=True),
        lax.all_to_all(restore(grads[2]), "seq", split_axis=0, concat_axis=1, tiled=True),
    )
    bias_part = jnp.sum(bias_part[:, None], axis=(1, 2))
    bias_total = lax.psum(lax.psum(bias_part, "seq"), "dp")
    bias_grad = bias_total / jnp.sqrt(jnp.float32(lax.axis_size("dp") * frame_count * patches))
    outputs = tuple(
        (
            jnp.concatenate(
                [spatial[number], returned[number].reshape(patches, temporal_cols)], axis=1
            )[None, None]
            for number in range(3)
        )
    )
    return (outputs[0], outputs[1], outputs[2], bias_grad)


def solution(mesh):
    return jax.shard_map(
        local,
        mesh=mesh,
        in_specs=(
            P("dp", "seq", None, None),
            P("dp", "seq", None, None),
            P("dp", "seq", None, None),
            P("dp", "seq", None, None),
            P(),
            P(),
        ),
        out_specs=(
            P("dp", "seq", None, None),
            P("dp", "seq", None, None),
            P("dp", "seq", None, None),
            P(),
        ),
        check_vma=False,
    )
```

profile of v0, /device:TPU:4, one launch (start us, length us, event | category | flops | bytes accessed | tf_op | source)
XLA Modules:
  0.0 374.6 jit_solution(15697160159344717763)
XLA Ops:
  0.6 1.9 copy.100
  6.1 11.6 %all-to-all-start = ((bf16[1,32,4,3072]{3,2,0,1:T(4,128)(2,1)}), bf16[1,32,4,3072]{3,2,0,1:T(4,128)(2,1)}, u32[]{:S(2)}, u32[]{:S(2)}) async-start(bf16[1,32,4,3072]{3,2,0,1:T(4,128)(2,1)} %bitcast.26), calls=%async_computation | async-start | bytes 1572864 | tf_op jit(solution)/shard_map/all_to_all | solution.py:86
  17.8 1.9 copy.101
  23.3 17.0 %all-to-all-done = bf16[1,32,4,3072]{3,2,0,1:T(4,128)(2,1)} async-done(((bf16[1,32,4,3072]{3,2,0,1:T(4,128)(2,1)}), bf16[1,32,4,3072]{3,2,0,1:T(4,128)(2,1)}, u32[]{:S(2)}, u32[]{:S(2)}) %all-to-all-start) | async-done | bytes 786464 | tf_op jit(solution)/shard_map/all_to_all | solution.py:86
  40.3 5.6 %all-to-all-start.1 = ((bf16[1,32,4,3072]{3,2,0,1:T(4,128)(2,1)}), bf16[1,32,4,3072]{3,2,0,1:T(4,128)(2,1)}, u32[]{:S(2)}, u32[]{:S(2)}) async-start(bf16[1,32,4,3072]{3,2,0,1:T(4,128)(2,1)} %bitcast.28), calls=%async_computation.1 | async-start | bytes 1572864 | tf_op jit(solution)/shard_map/all_to_all | solution.py:87
  54.8 12.4 %all-to-all-done.1 = bf16[1,32,4,3072]{3,2,0,1:T(4,128)(2,1)} async-done(((bf16[1,32,4,3072]{3,2,0,1:T(4,128)(2,1)}), bf16[1,32,4,3072]{3,2,0,1:T(4,128)(2,1)}, u32[]{:S(2)}, u32[]{:S(2)}) %all-to-all-start.1) | async-done | bytes 786464 | tf_op jit(solution)/shard_map/all_to_all | solution.py:87
  67.2 5.6 %all-to-all-start.3 = ((bf16[1,32,4,3072]{3,2,0,1:T(4,128)(2,1)}), bf16[1,32,4,3072]{3,2,0,1:T(4,128)(2,1)}, u32[]{:S(2)}, u32[]{:S(2)}) async-start(bf16[1,32,4,3072]{3,2,0,1:T(4,128)(2,1)} %bitcast.131), calls=%async_computation.3 | async-start | bytes 1572864 | tf_op jit(solution)/shard_map/all_to_all | solution.py:88
  75.4 18.3 %all-to-all-done.3 = bf16[1,32,4,3072]{3,2,0,1:T(4,128)(2,1)} async-done(((bf16[1,32,4,3072]{3,2,0,1:T(4,128)(2,1)}), bf16[1,32,4,3072]{3,2,0,1:T(4,128)(2,1)}, u32[]{:S(2)}, u32[]{:S(2)}) %all-to-all-start.3) | async-done | bytes 786464 | tf_op jit(solution)/shard_map/all_to_all | solution.py:88
  93.7 5.6 %all-to-all-start.2 = ((bf16[1,32,4,3072]{3,2,0,1:T(4,128)(2,1)}), bf16[1,32,4,3072]{3,2,0,1:T(4,128)(2,1)S(1)}, u32[]{:S(2)}, u32[]{:S(2)}) async-start(bf16[1,32,4,3072]{3,2,0,1:T(4,128)(2,1)} %bitcast.32), calls=%async_computation.2 | async-start | bytes 1572864 | tf_op jit(solution)/shard_map/all_to_all | solution.py:89
  103.6 2.6 reshape.216
  106.2 2.3 reshape.218
  108.6 4.0 %fusion.51 = (f32[4,24,32]{2,1,0:T(8,128)}, f32[4,24,32,32]{2,3,1,0:T(8,128)}) fusion(f32[24,32,32]{1,2,0:T(8,128)S(1)} %copy.121, pred[32]{0:T(512)(128)(4,1)S(1)} %iota_compare_fusion.1, bf16[32,4,24,128]{3,2,1,0:T(8,128)(2,1)} %reshape.216, bf16[32,4,24,128]{3,2,1,0:T(8,128)(2,1)S(1)} %reshape.215), kind=kOutput, calls=%fused_computation.66 | convolution fusion | flops 25657376 | bytes 2076704 | tf_op jit(solution)/shard_map/sub | solution.py:23
  112.6 7.4 %all-to-all-done.2 = bf16[1,32,4,3072]{3,2,0,1:T(4,128)(2,1)S(1)} async-done(((bf16[1,32,4,3072]{3,2,0,1:T(4,128)(2,1)}), bf16[1,32,4,3072]{3,2,0,1:T(4,128)(2,1)S(1)}, u32[]{:S(2)}, u32[]{:S(2)}) %all-to-all-start.2) | async-done | bytes 786464 | tf_op jit(solution)/shard_map/all_to_all | solution.py:89
  121.2 2.7 fusion.4
  123.9 2.1 subtract_multiply_fusion
  127.9 2.5 reshape.219
  130.3 5.6 %all-to-all-start.4 = ((bf16[32,1,4,3072]{3,2,1,0:T(4,128)(2,1)}), bf16[32,1,4,3072]{3,2,1,0:T(4,128)(2,1)}, u32[]{:S(2)}, u32[]{:S(2)}) async-start(bf16[32,1,4,3072]{3,2,1,0:T(4,128)(2,1)} %reshape.219), calls=%async_computation.4 | async-start | bytes 1572864 | tf_op jit(solution)/shard_map/all_to_all | solution.py:111
  135.9 2.5 copy.157
  140.3 3.1 multiply_reduce_fusion
  145.1 2.5 reshape.221
  147.5 8.8 %all-to-all-done.4 = bf16[32,1,4,3072]{3,2,1,0:T(4,128)(2,1)} async-done(((bf16[32,1,4,3072]{3,2,1,0:T(4,128)(2,1)}), bf16[32,1,4,3072]{3,2,1,0:T(4,128)(2,1)}, u32[]{:S(2)}, u32[]{:S(2)}) %all-to-all-start.4) | async-done | bytes 786464 | tf_op jit(solution)/shard_map/all_to_all | solution.py:111
  156.3 5.6 %all-to-all-start.6 = ((bf16[32,1,4,3072]{3,2,1,0:T(4,128)(2,1)}), bf16[32,1,4,3072]{3,2,1,0:T(4,128)(2,1)}, u32[]{:S(2)}, u32[]{:S(2)}) async-start(bf16[32,1,4,3072]{3,2,1,0:T(4,128)(2,1)} %reshape.221), calls=%async_computation.6 | async-start | bytes 1572864 | tf_op jit(solution)/shard_map/all_to_all | solution.py:113
  161.9 3.2 convolution_convert_fusion.1
  165.1 2.3 copy.143
  167.5 2.4 multiply_convert_fusion.4
  171.1 2.3 copy.135
  173.4 2.7 multiply_convert_fusion.1
  176.1 2.3 copy.139
  182.1 138.3 %psum.14 = f32[24,63]{1,0:T(8,128)S(1)} all-reduce(f32[24,63]{1,0:T(8,128)S(1)} %bitcast.141), channel_id=1, replica_groups=mesh['dp'=8,'seq'=32] {'seq'}, use_global_device_ids=true, to_apply=%region_5.6 | all-reduce | flops 1512 | bytes 12096 | tf_op jit(solution)/shard_map/psum | solution.py:116
  320.5 23.6 %psum.15 = f32[24,63]{1,0:T(8,128)S(1)} all-reduce(f32[24,63]{1,0:T(8,128)S(1)} %psum.14), channel_id=1, replica_groups=mesh['dp'=8,'seq'=32] {'dp'}, use_global_device_ids=true, to_apply=%region_6.7 | all-reduce | flops 1512 | bytes 12096 | tf_op jit(solution)/shard_map/psum | solution.py:116
  344.1 9.5 %all-to-all-start.5 = ((bf16[32,1,4,3072]{3,2,1,0:T(4,128)(2,1)}), bf16[32,1,4,3072]{3,2,1,0:T(4,128)(2,1)S(1)}, u32[]{:S(2)}, u32[]{:S(2)}) async-start(bf16[32,1,4,3072]{3,2,1,0:T(4,128)(2,1)} %reshape.220), calls=%async_computation.5 | async-start | bytes 1572864 | tf_op jit(solution)/shard_map/all_to_all | solution.py:112
  360.1 13.1 %all-to-all-done.5 = bf16[32,1,4,3072]{3,2,1,0:T(4,128)(2,1)S(1)} async-done(((bf16[32,1,4,3072]{3,2,1,0:T(4,128)(2,1)}), bf16[32,1,4,3072]{3,2,1,0:T(4,128)(2,1)S(1)}, u32[]{:S(2)}, u32[]{:S(2)}) %all-to-all-start.5) | async-done | bytes 786464 | tf_op jit(solution)/shard_map/all_to_all | solution.py:112
  (75 shorter events, 41.5 us)
Async XLA Ops:
  0.6 99.3 %copy-start = (f32[24,63]{1,0:T(8,128)S(1)}, f32[24,63]{1,0:T(8,128)}, u32[]{:S(2)}) copy-start(f32[24,63]{1,0:T(8,128)} %param.11) | copy-start | bytes 18148
  6.1 34.1 %all-to-all-start = ((bf16[1,32,4,3072]{3,2,0,1:T(4,128)(2,1)}), bf16[1,32,4,3072]{3,2,0,1:T(4,128)(2,1)}, u32[]{:S(2)}, u32[]{:S(2)}) async-start(bf16[1,32,4,3072]{3,2,0,1:T(4,128)(2,1)} %bitcast.26), calls=%async_computation | async-start | bytes 1572864 | tf_op jit(solution)/shard_map/all_to_all | solution.py:86
  22.1 23.8 %copy-start.13 = (s32[8]{0:T(128)S(1)}, s32[8]{0:T(128)}, u32[]{:S(2)}) copy-start(s32[8]{0:T(128)} %param.10) | copy-start | bytes 100
  40.3 26.9 %all-to-all-start.1 = ((bf16[1,32,4,3072]{3,2,0,1:T(4,128)(2,1)}), bf16[1,32,4,3072]{3,2,0,1:T(4,128)(2,1)}, u32[]{:S(2)}, u32[]{:S(2)}) async-start(bf16[1,32,4,3072]{3,2,0,1:T(4,128)(2,1)} %bitcast.28), calls=%async_computation.1 | async-start | bytes 1572864 | tf_op jit(solution)/shard_map/all_to_all | solution.py:87
  67.2 26.5 %all-to-all-start.3 = ((bf16[1,32,4,3072]{3,2,0,1:T(4,128)(2,1)}), bf16[1,32,4,3072]{3,2,0,1:T(4,128)(2,1)}, u32[]{:S(2)}, u32[]{:S(2)}) async-start(bf16[1,32,4,3072]{3,2,0,1:T(4,128)(2,1)} %bitcast.131), calls=%async_computation.3 | async-start | bytes 1572864 | tf_op jit(solution)/shard_map/all_to_all | solution.py:88
  93.7 26.3 %all-to-all-start.2 = ((bf16[1,32,4,3072]{3,2,0,1:T(4,128)(2,1)}), bf16[1,32,4,3072]{3,2,0,1:T(4,128)(2,1)S(1)}, u32[]{:S(2)}, u32[]{:S(2)}) async-start(bf16[1,32,4,3072]{3,2,0,1:T(4,128)(2,1)} %bitcast.32), calls=%async_computation.2 | async-start | bytes 1572864 | tf_op jit(solution)/shard_map/all_to_all | solution.py:89
  99.3 0.6 copy-start.11
  103.6 5.0 %copy-start.1 = (bf16[32,4,24,128]{3,2,1,0:T(8,128)(2,1)}, bf16[32,4,24,128]{3,2,1,0:T(8,128)(2,1)S(1)}, u32[]{:S(2)}) copy-start(bf16[32,4,24,128]{3,2,1,0:T(8,128)(2,1)S(1)} %reshape.215) | copy-start | bytes 2359300
  112.6 8.6 %copy-start.16 = (f32[4,24,32]{2,1,0:T(8,128)S(1)}, f32[4,24,32]{2,1,0:T(8,128)}, u32[]{:S(2)}) copy-start(f32[4,24,32]{2,1,0:T(8,128)} %get-tuple-element.12) | copy-start | bytes 36868
  120.3 0.9 copy-start.8
  121.2 2.7 copy-start.10
  121.2 2.7 copy-start.14
  123.9 2.1 copy-start.6
  130.3 26.0 %all-to-all-start.4 = ((bf16[32,1,4,3072]{3,2,1,0:T(4,128)(2,1)}), bf16[32,1,4,3072]{3,2,1,0:T(4,128)(2,1)}, u32[]{:S(2)}, u32[]{:S(2)}) async-start(bf16[32,1,4,3072]{3,2,1,0:T(4,128)(2,1)} %reshape.219), calls=%async_computation.4 | async-start | bytes 1572864 | tf_op jit(solution)/shard_map/all_to_all | solution.py:111
  140.3 3.1 copy-start.9
  140.3 3.1 copy-start.15
  156.3 187.8 %all-to-all-start.6 = ((bf16[32,1,4,3072]{3,2,1,0:T(4,128)(2,1)}), bf16[32,1,4,3072]{3,2,1,0:T(4,128)(2,1)}, u32[]{:S(2)}, u32[]{:S(2)}) async-start(bf16[32,1,4,3072]{3,2,1,0:T(4,128)(2,1)} %reshape.221), calls=%async_computation.6 | async-start | bytes 1572864 | tf_op jit(solution)/shard_map/all_to_all | solution.py:113
  169.8 1.3 copy-start.7
  173.4 5.0 %copy-start.2 = (bf16[32,4,24,128]{3,2,1,0:T(8,128)(2,1)S(1)}, bf16[32,4,24,128]{3,2,1,0:T(8,128)(2,1)}, u32[]{:S(2)}) copy-start(bf16[32,4,24,128]{3,2,1,0:T(8,128)(2,1)} %copy-done.1) | copy-start | bytes 2359300
  178.9 1.4 copy-start.12
  344.1 29.1 %all-to-all-start.5 = ((bf16[32,1,4,3072]{3,2,1,0:T(4,128)(2,1)}), bf16[32,1,4,3072]{3,2,1,0:T(4,128)(2,1)S(1)}, u32[]{:S(2)}, u32[]{:S(2)}) async-start(bf16[32,1,4,3072]{3,2,1,0:T(4,128)(2,1)} %reshape.220), calls=%async_computation.5 | async-start | bytes 1572864 | tf_op jit(solution)/shard_map/all_to_all | solution.py:112
  354.2 3.2 copy-start.3
  357.4 1.4 copy-start.5
  360.1 13.3 %copy-start.4 = (bf16[128,3072]{1,0:T(8,128)(2,1)S(1)}, bf16[128,3072]{1,0:T(8,128)(2,1)}, u32[]{:S(2)}) copy-start(bf16[128,3072]{1,0:T(8,128)(2,1)} %copy.139) | copy-start | bytes 2359300
where the time goes:
time: 376 us; the launch traced here: 375 us
  blocking collectives  162 us (43%)
  waiting for transfers between devices  76.9 us (20%)
  local copies, waits for them, and re-layouts  51.7 us (14%)
  starting transfers between devices  49.2 us (13%)
  matrix products  27.9 us (7%)
  other arithmetic  5.33 us (1%)
    psum x2, blocking collectives, local(): bias_total = lax.psum(lax.psum(bias_part, 'seq'), 'dp')  162 us
    all_to_all x1, waiting for transfers between devices, local(): lax.all_to_all(rows_values, 'seq', split_axis=1, concat_axis=0, tiled=True)  18.3 us
    all_to_all x1, waiting for transfers between devices, local(): lax.all_to_all(rows_query, 'seq', split_axis=1, concat_axis=0, tiled=True)  17 us
    all_to_all x1, waiting for transfers between devices, local(): lax.all_to_all(restore(grads[1]), 'seq', split_axis=0, concat_axis=1, til...  13.1 us
    all_to_all x1, waiting for transfers between devices, local(): lax.all_to_all(rows_keys, 'seq', split_axis=1, concat_axis=0, tiled=True)  12.4 us
    unnamed x39, local copies, waits for them, and re-layouts  11.7 us
    all_to_all x1, starting transfers between devices, local(): lax.all_to_all(rows_query, 'seq', split_axis=1, concat_axis=0, tiled=True)  11.6 us
    all_to_all x1, starting transfers between devices, local(): lax.all_to_all(restore(grads[1]), 'seq', split_axis=0, concat_axis=1, til...  9.48 us
  transfers between devices with their start and end apart: 7, of which 6 were waited for; matrix products, arithmetic and copies ran while one was open for 18% of the time, Pallas kernels for 0%

commit v1 on v0

v1 whole, which is shorter than its diff:
```python
import functools

import jax
import jax.numpy as jnp
from jax import lax
from jax.experimental import pallas as pl
from jax.experimental.pallas import tpu as pltpu
from jax.sharding import PartitionSpec as P

SHEADS = 24
THEADS = 24
HDIM = 128
ROWS = 8
HALVES = 2
HEADS_HERE = THEADS // HALVES
WIDTH = HEADS_HERE * HDIM
SPATIAL = SHEADS * HDIM
SPAN = 512
NEG = -1e30
WIDE = jnp.float32
LOW = jnp.bfloat16
SCALE = HDIM ** (-0.5)
MIB = 1024 * 1024

NT = (((1,), (1,)), ((), ()))
NN = (((1,), (0,)), ((), ()))
TN = (((0,), (0,)), ((), ()))


def dot(left, right, dims):
    return lax.dot_general(left, right, dims, preferred_element_type=WIDE)


def head_grads(query, keys, values, grad, extra):
    logits = dot(keys, query, NT) * SCALE
    if extra is not None:
        logits = logits + extra
    exponent = jnp.exp(logits - jnp.max(logits, axis=0, keepdims=True))
    attention = exponent * (1.0 / jnp.sum(exponent, axis=0, keepdims=True))
    grad_attention = dot(values, grad, NT)
    row_delta = jnp.sum(attention * grad_attention, axis=0, keepdims=True)
    grad_logits = attention * (grad_attention - row_delta)
    grad_low = grad_logits.astype(LOW)
    grad_query = (dot(grad_low, keys, TN) * SCALE).astype(LOW)
    grad_keys = (dot(grad_low, query, NN) * SCALE).astype(LOW)
    grad_values = dot(attention.astype(LOW), grad, NN).astype(LOW)
    return grad_query, grad_keys, grad_values, grad_logits


def pack_kernel(query, keys, values, grad, packed, sems):
    copies = []
    for number, source in enumerate((query, keys, values, grad)):
        for half in range(HALVES):
            copies.append(
                pltpu.make_async_copy(
                    source.at[:, :, pl.ds(SPATIAL + half * WIDTH, WIDTH)],
                    packed.at[:, half, number],
                    sems.at[number * HALVES + half],
                )
            )
    for copy in copies:
        copy.start()
    for copy in copies:
        copy.wait()


def unpack_kernel(back, query_in, keys_in, values_in, query, keys, values, sems):
    copies = []
    for number, target in enumerate((query, keys, values)):
        for half in range(HALVES):
            copies.append(
                pltpu.make_async_copy(
                    back.at[:, half, number],
                    target.at[:, :, pl.ds(SPATIAL + half * WIDTH, WIDTH)],
                    sems.at[number * HALVES + half],
                )
            )
    for copy in copies:
        copy.start()
    for copy in copies:
        copy.wait()


def spatial_kernel(heads, live, query, keys, values, grad, grad_query, grad_keys, grad_values):
    flag = live[0].astype(WIDE).astype(LOW)
    for head in range(heads):
        cols = pl.ds(head * HDIM, HDIM)
        outs = head_grads(
            query[:, cols], keys[:, cols], values[:, cols], grad[:, cols] * flag, None
        )
        grad_query[:, cols] = outs[0]
        grad_keys[:, cols] = outs[1]
        grad_values[:, cols] = outs[2]


def table_kernel(frame_count, length, seed, table):
    shape = (ROWS, frame_count * ROWS)
    for frame in range(frame_count):
        row = seed[0]
        moved = pltpu.roll(row, frame * ROWS, 1) if frame else row
        allowed = jnp.full(shape, frame, jnp.int32) < length[0]
        table[0, pl.ds(frame * ROWS, ROWS), :] = jnp.where(allowed, moved[:, : shape[1]], NEG)


def temporal_kernel(frame_count, length, tensors, table, grads, bias_part):
    tokens = frame_count * ROWS
    live_rows = lax.broadcasted_iota(jnp.int32, (tokens, HDIM), 0) < length[0] * ROWS

    def one_head(head):
        cols = pl.ds(pl.multiple_of(head * HDIM, HDIM), HDIM)
        query, keys, values, grad = (
            tensors[:, number, :, cols].reshape(tokens, HDIM) for number in range(4)
        )
        grad = jnp.where(live_rows, grad.astype(WIDE), 0.0).astype(LOW)
        outs = head_grads(query, keys, values, grad, table[head])
        for number in range(3):
            grads[:, number, :, cols] = outs[number].reshape(frame_count, ROWS, HDIM)
        terms = outs[3].reshape(frame_count, ROWS, tokens)
        parts = [
            jnp.concatenate([terms[frame], jnp.zeros((ROWS, SPAN - tokens), WIDE)], axis=1)
            for frame in range(frame_count)
        ]
        step = ROWS
        while len(parts) > 1:
            parts = [
                parts[at] + pltpu.roll(parts[at + 1], SPAN - step, 1)
                for at in range(0, len(parts), 2)
            ]
            step *= 2
        bias_part[head] = parts[0]

    def pair(at, carry):
        one_head(2 * at)
        one_head(2 * at + 1)
        return carry

    lax.fori_loop(0, HEADS_HERE // 2, pair, 0)


def spec(space):
    return pl.BlockSpec(memory_space=space)


def params(limit):
    return pltpu.CompilerParams(vmem_limit_bytes=limit * MIB)


def butterfly(value, axis):
    count = lax.axis_size(axis)
    step = 1
    while step < count:
        value = value + lax.ppermute(value, axis, [(at, at ^ step) for at in range(count)])
        step *= 2
    return value


def local(query, keys, values, grad_out, frames, bias):
    frame_count = lax.axis_size("seq")
    frame_index = lax.axis_index("seq")
    length = lax.dynamic_index_in_dim(frames, lax.axis_index("dp"), 0, keepdims=True)
    live = (frame_index < length).astype(jnp.int32)
    patches, columns = query.shape[2], query.shape[3]
    groups = patches // ROWS
    tokens = frame_count * ROWS
    flat = [tensor.reshape(patches, columns) for tensor in (query, keys, values, grad_out)]
    tiled = [tensor.reshape(groups, ROWS, columns) for tensor in flat]

    packed = pl.pallas_call(
        pack_kernel,
        out_shape=jax.ShapeDtypeStruct((groups, HALVES, 4, ROWS, WIDTH), LOW),
        in_specs=[spec(pltpu.HBM)] * 4,
        out_specs=spec(pltpu.VMEM),
        scratch_shapes=[pltpu.SemaphoreType.DMA((4 * HALVES,))],
        compiler_params=params(60),
        name="pack",
    )(*tiled)
    gathered = lax.all_to_all(
        packed.reshape(frame_count, 4, ROWS, WIDTH), "seq", split_axis=0, concat_axis=0, tiled=True
    )

    heads = 4
    block = pl.BlockSpec((patches, heads * HDIM), lambda at, live: (0, at))
    spatial = pl.pallas_call(
        functools.partial(spatial_kernel, heads),
        out_shape=[jax.ShapeDtypeStruct((patches, columns), LOW)] * 3,
        grid_spec=pltpu.PrefetchScalarGridSpec(
            num_scalar_prefetch=1,
            grid=(SHEADS // heads,),
            in_specs=[block] * 4,
            out_specs=[block] * 3,
        ),
        compiler_params=params(48),
        cost_estimate=pl.CostEstimate(
            flops=10 * SHEADS * patches * patches * HDIM,
            bytes_accessed=14 * patches * SPATIAL,
            transcendentals=SHEADS * patches * patches,
        ),
        name="spatial",
    )(live, *flat)

    half = frame_index % HALVES
    bias_here = lax.dynamic_slice_in_dim(bias, half * HEADS_HERE, HEADS_HERE, 0)
    offsets = jnp.concatenate(
        [
            bias_here[:, :frame_count][:, ::-1],
            jnp.full((HEADS_HERE, 1), NEG, WIDE),
            bias_here[:, frame_count:][:, ::-1],
        ],
        axis=1,
    )
    seed = jnp.where(
        jnp.eye(ROWS, dtype=bool)[None, :, None, :], offsets[:, None, :, None], NEG
    ).reshape(HEADS_HERE, ROWS, SPAN)
    table = pl.pallas_call(
        functools.partial(table_kernel, frame_count),
        out_shape=jax.ShapeDtypeStruct((HEADS_HERE, tokens, tokens), WIDE),
        grid_spec=pltpu.PrefetchScalarGridSpec(
            num_scalar_prefetch=1,
            grid=(HEADS_HERE,),
            in_specs=[pl.BlockSpec((1, ROWS, SPAN), lambda at, length: (at, 0, 0))],
            out_specs=pl.BlockSpec((1, tokens, tokens), lambda at, length: (at, 0, 0)),
        ),
        compiler_params=params(48),
        cost_estimate=pl.CostEstimate(
            flops=HEADS_HERE * tokens * tokens * 4,
            bytes_accessed=HEADS_HERE * tokens * tokens * 4,
            transcendentals=0,
        ),
        name="table",
    )(length, seed)

    gathered, table, *spatial = lax.optimization_barrier((gathered, table, *spatial))
    grads, bias_part = pl.pallas_call(
        functools.partial(temporal_kernel, frame_count),
        out_shape=[
            jax.ShapeDtypeStruct((frame_count, 3, ROWS, WIDTH), LOW),
            jax.ShapeDtypeStruct((HEADS_HERE, ROWS, SPAN), WIDE),
        ],
        in_specs=[spec(pltpu.SMEM), spec(pltpu.VMEM), spec(pltpu.VMEM)],
        out_specs=[spec(pltpu.VMEM), spec(pltpu.VMEM)],
        compiler_params=params(48),
        cost_estimate=pl.CostEstimate(
            flops=10 * HEADS_HERE * tokens * tokens * HDIM,
            bytes_accessed=14 * tokens * WIDTH + 4 * HEADS_HERE * tokens * tokens,
            transcendentals=HEADS_HERE * tokens * tokens,
        ),
        name="temporal",
    )(length, gathered, table)

    back = lax.all_to_all(grads, "seq", split_axis=0, concat_axis=0, tiled=True)

    offset_sums = jnp.sum(
        bias_part.reshape(HEADS_HERE, ROWS, SPAN // ROWS, ROWS), axis=(1, 3)
    )
    sums = lax.dynamic_update_slice_in_dim(
        jnp.zeros((THEADS, SPAN // ROWS), WIDE), offset_sums, half * HEADS_HERE, 0
    )
    total = butterfly(butterfly(sums, "dp"), "seq")
    ordered = jnp.concatenate(
        [total[:, :frame_count][:, ::-1], total[:, frame_count + 1 :][:, ::-1]], axis=1
    )
    bias_grad = ordered / jnp.sqrt(WIDE(lax.axis_size("dp") * frame_count * patches))

    outputs = pl.pallas_call(
        unpack_kernel,
        out_shape=[jax.ShapeDtypeStruct((groups, ROWS, columns), LOW)] * 3,
        in_specs=[spec(pl.ANY)] + [spec(pltpu.HBM)] * 3,
        out_specs=[spec(pltpu.HBM)] * 3,
        scratch_shapes=[pltpu.SemaphoreType.DMA((3 * HALVES,))],
        input_output_aliases={1: 0, 2: 1, 3: 2},
        compiler_params=params(48),
        name="unpack",
    )(
        back.reshape(groups, HALVES, 3, ROWS, WIDTH),
        *(tensor.reshape(groups, ROWS, columns) for tensor in spatial),
    )
    shaped = tuple(tensor.reshape(1, 1, patches, columns) for tensor in outputs)
    return (*shaped, bias_grad)


def solution(mesh):
    split = P("dp", "seq", None, None)
    return jax.shard_map(
        local,
        mesh=mesh,
        in_specs=(split, split, split, split, P(), P()),
        out_specs=(split, split, split, P()),
        check_vma=False,
    )
```

time: 376 us -> 173 us (0.46)
  blocking collectives: 162 us -> 0 us
  local copies, waits for them, and re-layouts: 51.7 us -> 7.46 us
  matrix products: 27.9 us -> 0 us
  Pallas kernels: 0 us -> 26.9 us
  waiting for transfers between devices: 76.9 us -> 103 us
  starting transfers between devices: 49.2 us -> 32.3 us
    psum x2 -> x0, blocking collectives: 162 us -> none  [local(): bias_total = lax.psum(lax.psum(bias_part, 'seq'), 'dp')]
    ppermute x0 -> x8, waiting for transfers between devices: none -> 50.3 us  [butterfly(): lax.ppermute(value, axis, [(at, at ^ step) for at in range(count)])]
    reshape x20 -> x0, local copies, waits for them, and re-layouts: 30.6 us -> none  [the longest x6 8.68 us: restore(): jnp.transpose(tensor, (1, 0, 2, 3))]
    all_to_all x7 -> x2, starting transfers between devices: 49.2 us -> 19.1 us  [the longest x1 11.6 us: local(): lax.all_to_all(packed.reshape(frame_count, 4, ROWS, WIDTH), 'seq', split_...]
    pallas_call x0 -> x5, Pallas kernels: none -> 26.9 us  [the longest x1 9.96 us: local(): pl.pallas_call(functools.partial(temporal_kernel, frame_count), out_shape...]
    all_to_all x7 -> x2, waiting for transfers between devices: 76.9 us -> 52.3 us  [the longest x1 52.3 us: local(): lax.all_to_all(packed.reshape(frame_count, 4, ROWS, WIDTH), 'seq', split_...]
    dot_general x12 -> x0, matrix products: 22 us -> none  [the longest x2 5.81 us: attend_grads(): jnp.einsum('bhqk,bkhd->bqhd', attention_low, values, preferred_element_ty...]
    ppermute x0 -> x8, starting transfers between devices: none -> 13.2 us  [butterfly(): lax.ppermute(value, axis, [(at, at ^ step) for at in range(count)])]
  transfers between devices with their start and end apart: 7 -> 10, of which waited for: 6 -> 9; matrix products, arithmetic and copies ran while one was open for 18% -> 3% of each run, Pallas kernels for 0% -> 7%
where the time goes in v1:
time: 173 us
  waiting for transfers between devices  103 us (60%)
  starting transfers between devices  32.3 us (19%)
  Pallas kernels  26.9 us (16%)
  local copies, waits for them, and re-layouts  7.46 us (4%)
  other arithmetic  1.82 us (1%)
    all_to_all x1, waiting for transfers between devices, local(): lax.all_to_all(packed.reshape(frame_count, 4, ROWS, WIDTH), 'seq', split_...  52.3 us
    ppermute x8, waiting for transfers between devices, butterfly(): lax.ppermute(value, axis, [(at, at ^ step) for at in range(count)])  50.3 us
    ppermute x8, starting transfers between devices, butterfly(): lax.ppermute(value, axis, [(at, at ^ step) for at in range(count)])  13.2 us
    all_to_all x1, starting transfers between devices, local(): lax.all_to_all(packed.reshape(frame_count, 4, ROWS, WIDTH), 'seq', split_...  11.6 us
    pallas_call x1, Pallas kernels, local(): pl.pallas_call(functools.partial(temporal_kernel, frame_count), out_shape...  9.96 us
    pallas_call x1, Pallas kernels, local(): pl.pallas_call(functools.partial(spatial_kernel, heads), out_shape=[jax.S...  9.1 us
    all_to_all x1, starting transfers between devices, local(): back = lax.all_to_all(grads, 'seq', split_axis=0, concat_axis=0, tiled=True)  7.48 us
    unnamed x14, local copies, waits for them, and re-layouts  4.55 us
  transfers between devices with their start and end apart: 10, of which 9 were waited for; matrix products, arithmetic and copies ran while one was open for 3% of the time, Pallas kernels for 7%

profile of v1, /device:TPU:4, one launch (start us, length us, event | category | flops | bytes accessed | tf_op | source)
XLA Modules:
  0.0 172.6 jit_solution(14551989548327577901)
XLA Ops:
  0.6 3.6 %pack.1 = bf16[16,2,4,8,1536]{4,3,2,1,0:T(8,128)(2,1)} custom-call(bf16[16,8,6144]{2,1,0:T(8,128)(2,1)} %bitcast.20, bf16[16,8,6144]{2,1,0:T(8,128)(2,1)} %bitcast.22, bf16[16,8,6144]{2,1,0:T(8,128)(2,1)} %bitcast.24, bf16[16,8,6144]{2,1,0:T(8,128)(2,1)} %bitcast.27), custom_call_target="tpu_custom_call" | custom-call | tf_op jit(solution)/shard_map/pack/pallas_call | solution.py:168
  4.2 11.6 %all-to-all-start = ((bf16[32,4,8,1536]{3,2,1,0:T(8,128)(2,1)}), bf16[32,4,8,1536]{3,2,1,0:T(8,128)(2,1)S(1)}, u32[]{:S(2)}, u32[]{:S(2)}) async-start(bf16[32,4,8,1536]{3,2,1,0:T(8,128)(2,1)} %bitcast.26), calls=%async_computation | async-start | bytes 6291456 | tf_op jit(solution)/shard_map/all_to_all | solution.py:177
  16.4 0.8 broadcast_in_dim.37
  17.3 0.2 broadcast_in_dim.34
  17.5 0.6 dynamic_slice.7.length
  18.7 0.8 broadcast_select_fusion.seed
  19.6 2.8 %table.1 = f32[12,256,256]{2,1,0:T(8,128)S(1)} custom-call(s32[1]{0:T(128)} %dynamic_slice.7.length, f32[12,8,512]{2,1,0:T(8,128)S(1)} %broadcast_select_fusion.seed), custom_call_target="tpu_custom_call" | custom-call | flops 3145728 | bytes 3145728 | tf_op jit(solution)/shard_map/table/pallas_call | solution.py:214
  22.4 1.7 copy-done
  24.1 1.4 copy-done.3
  25.5 9.1 %spatial.1 = (bf16[128,6144]{1,0:T(8,128)(2,1)}, bf16[128,6144]{1,0:T(8,128)(2,1)}, bf16[128,6144]{1,0:T(8,128)(2,1)}) custom-call(s32[1]{0:T(128)S(6)} %convert_element_type.3.live, bf16[128,6144]{1,0:T(8,128)(2,1)S(1)} %bitcast.21, bf16[128,6144]{1,0:T(8,128)(2,1)S(1)} %bitcast.23, bf16[128,6144]{1,0:T(8,128)(2,1)S(1)} %bitcast.25, bf16[128,6144]{1,0:T(8,128)(2,1)} %bitcast.28), custom_call_target="tpu_custom_call" | custom-call | flops 503316480 | bytes 5505024 | tf_op jit(solution)/shard_map/spatial/pallas_call | solution.py:183
  34.6 52.3 %all-to-all-done.tensors = bf16[32,4,8,1536]{3,2,1,0:T(8,128)(2,1)S(1)} async-done(((bf16[32,4,8,1536]{3,2,1,0:T(8,128)(2,1)}), bf16[32,4,8,1536]{3,2,1,0:T(8,128)(2,1)S(1)}, u32[]{:S(2)}, u32[]{:S(2)}) %all-to-all-start) | async-done | bytes 3145760 | tf_op jit(solution)/shard_map/all_to_all | solution.py:177
  86.9 10.0 %temporal.1 = (bf16[32,3,8,1536]{3,2,1,0:T(8,128)(2,1)S(1)}, f32[12,8,512]{2,1,0:T(8,128)S(1)}) custom-call(s32[1]{0:T(128)} %dynamic_slice.7.length, bf16[32,4,8,1536]{3,2,1,0:T(8,128)(2,1)S(1)} %all-to-all-done.tensors, f32[12,256,256]{2,1,0:T(8,128)} %copy-done), custom_call_target="tpu_custom_call" | custom-call | flops 1006632960 | bytes 8650752 | tf_op jit(solution)/shard_map/temporal/pallas_call | solution.py:233
  96.9 1.4 copy-done.4
  98.3 7.5 %all-to-all-start.1 = ((bf16[32,3,8,1536]{3,2,1,0:T(8,128)(2,1)}), bf16[32,3,8,1536]{3,2,1,0:T(8,128)(2,1)S(1)}, u32[]{:S(2)}, u32[]{:S(2)}) async-start(bf16[32,3,8,1536]{3,2,1,0:T(8,128)(2,1)} %copy-done.4), calls=%async_computation.1 | async-start | bytes 4718592 | tf_op jit(solution)/shard_map/all_to_all | solution.py:250
  105.9 0.2 reduce_sum.14
  106.6 1.2 collective-permute-done
  107.9 1.7 collective-permute-start.1
  109.6 2.1 %collective-permute-done.1 = f32[24,64]{1,0:T(8,128)S(1)} collective-permute-done((f32[24,64]{1,0:T(8,128)S(1)}, f32[24,64]{1,0:T(8,128)S(1)}, u32[]{:S(2)}, u32[]{:S(2)}) %collective-permute-start.1) | collective-permute-done | bytes 6176 | tf_op jit(solution)/shard_map/ppermute | solution.py:152
  111.7 3.2 %collective-permute-start.2 = (f32[24,64]{1,0:T(8,128)S(1)}, f32[24,64]{1,0:T(8,128)S(1)}, u32[]{:S(2)}, u32[]{:S(2)}) collective-permute-start(f32[24,64]{1,0:T(8,128)S(1)} %add.41), channel_id=1, source_target_pairs={{0,128},{32,160},{64,192},{96,224},{128,0},{160,32},{192,64},{224,... | collective-permute-start | bytes 18440 | tf_op jit(solution)/shard_map/ppermute | solution.py:152
  114.9 2.0 %collective-permute-done.2 = f32[24,64]{1,0:T(8,128)S(1)} collective-permute-done((f32[24,64]{1,0:T(8,128)S(1)}, f32[24,64]{1,0:T(8,128)S(1)}, u32[]{:S(2)}, u32[]{:S(2)}) %collective-permute-start.2) | collective-permute-done | bytes 6176 | tf_op jit(solution)/shard_map/ppermute | solution.py:152
  116.9 1.1 collective-permute-start.3
  118.1 2.6 %collective-permute-done.3 = f32[24,64]{1,0:T(8,128)S(1)} collective-permute-done((f32[24,64]{1,0:T(8,128)S(1)}, f32[24,64]{1,0:T(8,128)S(1)}, u32[]{:S(2)}, u32[]{:S(2)}) %collective-permute-start.3) | collective-permute-done | bytes 6176 | tf_op jit(solution)/shard_map/ppermute | solution.py:152
  120.7 0.2 collective-permute-start.4
  121.0 5.0 %collective-permute-done.4 = f32[24,64]{1,0:T(8,128)S(1)} collective-permute-done((f32[24,64]{1,0:T(8,128)S(1)}, f32[24,64]{1,0:T(8,128)S(1)}, u32[]{:S(2)}, u32[]{:S(2)}) %collective-permute-start.4) | collective-permute-done | bytes 6176 | tf_op jit(solution)/shard_map/ppermute | solution.py:152
  126.0 1.5 collective-permute-start.5
  127.5 30.5 %collective-permute-done.5 = f32[24,64]{1,0:T(8,128)S(1)} collective-permute-done((f32[24,64]{1,0:T(8,128)S(1)}, f32[24,64]{1,0:T(8,128)S(1)}, u32[]{:S(2)}, u32[]{:S(2)}) %collective-permute-start.5) | collective-permute-done | bytes 6176 | tf_op jit(solution)/shard_map/ppermute | solution.py:152
  158.0 0.9 collective-permute-start.6
  158.9 3.7 %collective-permute-done.6 = f32[24,64]{1,0:T(8,128)S(1)} collective-permute-done((f32[24,64]{1,0:T(8,128)S(1)}, f32[24,64]{1,0:T(8,128)S(1)}, u32[]{:S(2)}, u32[]{:S(2)}) %collective-permute-start.6) | collective-permute-done | bytes 6176 | tf_op jit(solution)/shard_map/ppermute | solution.py:152
  162.6 4.5 %collective-permute-start.7 = (f32[24,64]{1,0:T(8,128)S(1)}, f32[24,64]{1,0:T(8,128)S(1)}, u32[]{:S(2)}, u32[]{:S(2)}) collective-permute-start(f32[24,64]{1,0:T(8,128)S(1)} %add.46), channel_id=1, source_target_pairs={{0,16},{1,17},{2,18},{3,19},{4,20},{5,21},{6,22},{7,23},{8,24},{9,... | collective-permute-start | bytes 18440 | tf_op jit(solution)/shard_map/ppermute | solution.py:152
  167.1 3.1 %collective-permute-done.7 = f32[24,64]{1,0:T(8,128)S(1)} collective-permute-done((f32[24,64]{1,0:T(8,128)S(1)}, f32[24,64]{1,0:T(8,128)S(1)}, u32[]{:S(2)}, u32[]{:S(2)}) %collective-permute-start.7) | collective-permute-done | bytes 6176 | tf_op jit(solution)/shard_map/ppermute | solution.py:152
  170.4 0.7 maximum_multiply_fusion
  171.1 1.4 unpack.1
  (38 shorter events, 1.5 us)
Async XLA Ops:
  4.2 11.7 %copy-start.5 = (f32[24,63]{1,0:T(8,128)S(1)}, f32[24,63]{1,0:T(8,128)}, u32[]{:S(2)}) copy-start(f32[24,63]{1,0:T(8,128)} %param.11) | copy-start | bytes 18148
  4.2 13.3 %copy-start.6 = (s32[8]{0:T(128)S(1)}, s32[8]{0:T(128)}, u32[]{:S(2)}) copy-start(s32[8]{0:T(128)} %param.10) | copy-start | bytes 100
  4.2 82.7 %all-to-all-start = ((bf16[32,4,8,1536]{3,2,1,0:T(8,128)(2,1)}), bf16[32,4,8,1536]{3,2,1,0:T(8,128)(2,1)S(1)}, u32[]{:S(2)}, u32[]{:S(2)}) async-start(bf16[32,4,8,1536]{3,2,1,0:T(8,128)(2,1)} %bitcast.26), calls=%async_computation | async-start | bytes 6291456 | tf_op jit(solution)/shard_map/all_to_all | solution.py:177
  19.5 4.6 %copy-start.1 = (bf16[1,1,128,6144]{3,2,1,0:T(8,128)(2,1)S(1)}, bf16[1,1,128,6144]{3,2,1,0:T(8,128)(2,1)}, u32[]{:S(2)}) copy-start(bf16[1,1,128,6144]{3,2,1,0:T(8,128)(2,1)} %param.6) | copy-start | bytes 4718596
  19.6 4.5 %copy-start.2 = (bf16[1,1,128,6144]{3,2,1,0:T(8,128)(2,1)S(1)}, bf16[1,1,128,6144]{3,2,1,0:T(8,128)(2,1)}, u32[]{:S(2)}) copy-start(bf16[1,1,128,6144]{3,2,1,0:T(8,128)(2,1)} %param.7) | copy-start | bytes 4718596
  22.4 1.7 copy-start
  24.1 1.4 copy-start.3
  96.9 1.4 copy-start.4
  98.3 72.8 %all-to-all-start.1 = ((bf16[32,3,8,1536]{3,2,1,0:T(8,128)(2,1)}), bf16[32,3,8,1536]{3,2,1,0:T(8,128)(2,1)S(1)}, u32[]{:S(2)}, u32[]{:S(2)}) async-start(bf16[32,3,8,1536]{3,2,1,0:T(8,128)(2,1)} %copy-done.4), calls=%async_computation.1 | async-start | bytes 4718592 | tf_op jit(solution)/shard_map/all_to_all | solution.py:250
  106.5 1.3 collective-permute-start
  107.9 3.8 %collective-permute-start.1 = (f32[24,64]{1,0:T(8,128)S(1)}, f32[24,64]{1,0:T(8,128)S(1)}, u32[]{:S(2)}, u32[]{:S(2)}) collective-permute-start(f32[24,64]{1,0:T(8,128)S(1)} %add.40), channel_id=1, source_target_pairs={{0,64},{32,96},{64,0},{96,32},{128,192},{160,224},{192,128},{224,1... | collective-permute-start | bytes 18440 | tf_op jit(solution)/shard_map/ppermute | solution.py:152
  111.7 5.2 %collective-permute-start.2 = (f32[24,64]{1,0:T(8,128)S(1)}, f32[24,64]{1,0:T(8,128)S(1)}, u32[]{:S(2)}, u32[]{:S(2)}) collective-permute-start(f32[24,64]{1,0:T(8,128)S(1)} %add.41), channel_id=1, source_target_pairs={{0,128},{32,160},{64,192},{96,224},{128,0},{160,32},{192,64},{224,... | collective-permute-start | bytes 18440 | tf_op jit(solution)/shard_map/ppermute | solution.py:152
  116.9 3.8 %collective-permute-start.3 = (f32[24,64]{1,0:T(8,128)S(1)}, f32[24,64]{1,0:T(8,128)S(1)}, u32[]{:S(2)}, u32[]{:S(2)}) collective-permute-start(f32[24,64]{1,0:T(8,128)S(1)} %add.42), channel_id=1, source_target_pairs={{0,1},{1,0},{2,3},{3,2},{4,5},{5,4},{6,7},{7,6},{8,9},{9,8},{10,11... | collective-permute-start | bytes 18440 | tf_op jit(solution)/shard_map/ppermute | solution.py:152
  120.7 5.3 %collective-permute-start.4 = (f32[24,64]{1,0:T(8,128)S(1)}, f32[24,64]{1,0:T(8,128)S(1)}, u32[]{:S(2)}, u32[]{:S(2)}) collective-permute-start(f32[24,64]{1,0:T(8,128)S(1)} %add.43), channel_id=1, source_target_pairs={{0,2},{1,3},{2,0},{3,1},{4,6},{5,7},{6,4},{7,5},{8,10},{9,11},{10,... | collective-permute-start | bytes 18440 | tf_op jit(solution)/shard_map/ppermute | solution.py:152
  126.0 32.0 %collective-permute-start.5 = (f32[24,64]{1,0:T(8,128)S(1)}, f32[24,64]{1,0:T(8,128)S(1)}, u32[]{:S(2)}, u32[]{:S(2)}) collective-permute-start(f32[24,64]{1,0:T(8,128)S(1)} %add.44), channel_id=1, source_target_pairs={{0,4},{1,5},{2,6},{3,7},{4,0},{5,1},{6,2},{7,3},{8,12},{9,13},{10,... | collective-permute-start | bytes 18440 | tf_op jit(solution)/shard_map/ppermute | solution.py:152
  158.0 4.6 %collective-permute-start.6 = (f32[24,64]{1,0:T(8,128)S(1)}, f32[24,64]{1,0:T(8,128)S(1)}, u32[]{:S(2)}, u32[]{:S(2)}) collective-permute-start(f32[24,64]{1,0:T(8,128)S(1)} %add.45), channel_id=1, source_target_pairs={{0,8},{1,9},{2,10},{3,11},{4,12},{5,13},{6,14},{7,15},{8,0},{9,1},... | collective-permute-start | bytes 18440 | tf_op jit(solution)/shard_map/ppermute | solution.py:152
  162.6 7.6 %collective-permute-start.7 = (f32[24,64]{1,0:T(8,128)S(1)}, f32[24,64]{1,0:T(8,128)S(1)}, u32[]{:S(2)}, u32[]{:S(2)}) collective-permute-start(f32[24,64]{1,0:T(8,128)S(1)} %add.46), channel_id=1, source_target_pairs={{0,16},{1,17},{2,18},{3,19},{4,20},{5,21},{6,22},{7,23},{8,24},{9,... | collective-permute-start | bytes 18440 | tf_op jit(solution)/shard_map/ppermute | solution.py:152

commit v2 on v1

v2 whole, which is shorter than its diff:
```python
import functools

import jax
import jax.numpy as jnp
from jax import lax
from jax.experimental import pallas as pl
from jax.experimental.pallas import tpu as pltpu
from jax.sharding import PartitionSpec as P

SHEADS = 24
THEADS = 24
HDIM = 128
ROWS = 8
HALVES = 2
HEADS_HERE = THEADS // HALVES
WIDTH = HEADS_HERE * HDIM
SPATIAL = SHEADS * HDIM
SPAN = 512
NEG = -1e30
LOG2E = 1.4426950408889634
WIDE = jnp.float32
LOW = jnp.bfloat16
SCALE = HDIM ** (-0.5)
MIB = 1024 * 1024

NT = (((1,), (1,)), ((), ()))
NN = (((1,), (0,)), ((), ()))
TN = (((0,), (0,)), ((), ()))


def dot(left, right, dims):
    return lax.dot_general(left, right, dims, preferred_element_type=WIDE)


def head_grads(query, keys, values, grad, extra):
    logits = dot(keys, query, NT) * (SCALE * LOG2E)
    if extra is not None:
        logits = logits + extra
    exponent = jnp.exp2(logits - jnp.max(logits, axis=0, keepdims=True))
    attention = exponent * (1.0 / jnp.sum(exponent, axis=0, keepdims=True))
    grad_attention = dot(values, grad, NT)
    row_delta = jnp.sum(attention * grad_attention, axis=0, keepdims=True)
    grad_logits = attention * (grad_attention - row_delta)
    grad_low = grad_logits.astype(LOW)
    grad_query = (dot(grad_low, keys, TN) * SCALE).astype(LOW)
    grad_keys = (dot(grad_low, query, NN) * SCALE).astype(LOW)
    grad_values = dot(attention.astype(LOW), grad, NN).astype(LOW)
    return grad_query, grad_keys, grad_values, grad_logits


def pack_kernel(query, keys, values, grad, packed, staged, in_sems, out_sems):
    reads, writes = [], []
    for number, source in enumerate((query, keys, values, grad)):
        for half in range(HALVES):
            at = number * HALVES + half
            reads.append(
                pltpu.make_async_copy(
                    source.at[:, :, pl.ds(SPATIAL + half * WIDTH, WIDTH)],
                    staged.at[:, half, number],
                    in_sems.at[at],
                )
            )
            writes.append(
                pltpu.make_async_copy(
                    staged.at[:, half, number], packed.at[:, half, number], out_sems.at[at]
                )
            )
    for copy in reads:
        copy.start()
    for read, write in zip(reads, writes):
        read.wait()
        write.start()
    for copy in writes:
        copy.wait()


def unpack_kernel(back, query_in, keys_in, values_in, query, keys, values, sems):
    copies = []
    for number, target in enumerate((query, keys, values)):
        for half in range(HALVES):
            copies.append(
                pltpu.make_async_copy(
                    back.at[:, half, number],
                    target.at[:, :, pl.ds(SPATIAL + half * WIDTH, WIDTH)],
                    sems.at[number * HALVES + half],
                )
            )
    for copy in copies:
        copy.start()
    for copy in copies:
        copy.wait()


def spatial_kernel(heads, live, query, keys, values, grad, grad_query, grad_keys, grad_values):
    flag = live[0].astype(WIDE).astype(LOW)
    for head in range(heads):
        cols = pl.ds(head * HDIM, HDIM)
        outs = head_grads(
            query[:, cols], keys[:, cols], values[:, cols], grad[:, cols] * flag, None
        )
        grad_query[:, cols] = outs[0]
        grad_keys[:, cols] = outs[1]
        grad_values[:, cols] = outs[2]


def moved_rows(seed, frame_count, length):
    blocks = SPAN // HDIM
    turns = HDIM // ROWS
    wide = frame_count * ROWS // HDIM
    rows = [None] * frame_count
    for turn in range(turns):
        moved = pltpu.roll(seed, turn * ROWS, 1) if turn else seed
        pieces = [moved[:, at * HDIM : (at + 1) * HDIM] for at in range(blocks)]
        for frame in range(turn, frame_count, turns):
            shift = frame // turns
            joined = jnp.concatenate([pieces[(at - shift) % blocks] for at in range(wide)], axis=1)
            rows[frame] = jnp.where(frame < length, joined, NEG)
    return jnp.concatenate(rows, axis=0)


def offset_sums(terms, frame_count):
    blocks = SPAN // HDIM
    turns = HDIM // ROWS
    wide = frame_count * ROWS // HDIM
    parts = []
    for turn in range(turns):
        pieces = [None] * blocks
        for frame in range(turn, frame_count, turns):
            for at in range(wide):
                to = (at - frame // turns) % blocks
                piece = terms[frame][:, at * HDIM : (at + 1) * HDIM]
                pieces[to] = piece if pieces[to] is None else pieces[to] + piece
        pieces = [jnp.zeros((ROWS, HDIM), WIDE) if piece is None else piece for piece in pieces]
        parts.append(jnp.concatenate(pieces, axis=1))
    step = ROWS
    while len(parts) > 1:
        parts = [
            parts[at] + pltpu.roll(parts[at + 1], SPAN - step, 1)
            for at in range(0, len(parts), 2)
        ]
        step *= 2
    return parts[0]


def temporal_kernel(
    frame_count, heads, length, tensors, seed, grads, bias_part, staged, sems
):
    tokens = frame_count * ROWS
    live_rows = lax.broadcasted_iota(jnp.int32, (tokens, HDIM), 0) < length[0] * ROWS

    def one_head(head):
        cols = pl.ds(pl.multiple_of(head * HDIM, HDIM), HDIM)
        query, keys, values, grad = (
            tensors[:, number, :, cols].reshape(tokens, HDIM) for number in range(4)
        )
        grad = jnp.where(live_rows, grad.astype(WIDE), 0.0).astype(LOW)
        table = moved_rows(seed[head], frame_count, length[0])
        outs = head_grads(query, keys, values, grad, table)
        for number in range(3):
            staged[:, number, :, cols] = outs[number].reshape(frame_count, ROWS, HDIM)
        terms = outs[3].reshape(frame_count, ROWS, tokens)
        bias_part[head] = offset_sums(terms, frame_count)

    def write(at):
        cols = pl.ds(pl.multiple_of(at * heads * HDIM, HDIM), heads * HDIM)
        return pltpu.make_async_copy(
            staged.at[:, :, :, cols], grads.at[:, :, :, cols], sems.at[at]
        )

    def step(at, carry):
        for offset in range(heads):
            one_head(at * heads + offset)
        write(at).start()
        return carry

    def finish(at, carry):
        write(at).wait()
        return carry

    lax.fori_loop(0, HEADS_HERE // heads, step, 0)
    lax.fori_loop(0, HEADS_HERE // heads, finish, 0)


def spec(space):
    return pl.BlockSpec(memory_space=space)


def place(space, *arrays):
    return [pltpu.with_memory_space_constraint(array, space) for array in arrays]


def params(limit):
    return pltpu.CompilerParams(vmem_limit_bytes=limit * MIB)


def exchange_sum(value, axis, steps):
    count = lax.axis_size(axis)
    pieces = [value] + [
        lax.ppermute(value, axis, [(at, at ^ step) for at in range(count)]) for step in steps
    ]
    while len(pieces) > 1:
        pieces = [pieces[at] + pieces[at + 1] for at in range(0, len(pieces), 2)]
    return pieces[0]


def local(query, keys, values, grad_out, frames, bias):
    frame_count = lax.axis_size("seq")
    frame_index = lax.axis_index("seq")
    length = lax.dynamic_index_in_dim(frames, lax.axis_index("dp"), 0, keepdims=True)
    live = (frame_index < length).astype(jnp.int32)
    patches, columns = query.shape[2], query.shape[3]
    groups = patches // ROWS
    tokens = frame_count * ROWS
    flat = [tensor.reshape(patches, columns) for tensor in (query, keys, values, grad_out)]
    tiled = [tensor.reshape(groups, ROWS, columns) for tensor in flat]

    packed = pl.pallas_call(
        pack_kernel,
        out_shape=pltpu.HBM((groups, HALVES, 4, ROWS, WIDTH), LOW),
        in_specs=[spec(pl.ANY)] * 4,
        out_specs=spec(pl.ANY),
        scratch_shapes=[
            pltpu.VMEM((groups, HALVES, 4, ROWS, WIDTH), LOW),
            pltpu.SemaphoreType.DMA((4 * HALVES,)),
            pltpu.SemaphoreType.DMA((4 * HALVES,)),
        ],
        compiler_params=params(8),
        name="pack",
    )(*place(pltpu.HBM, *tiled))
    gathered = lax.all_to_all(
        packed.reshape(frame_count, 4, ROWS, WIDTH), "seq", split_axis=0, concat_axis=0, tiled=True
    )

    heads = 4
    block = pl.BlockSpec((patches, heads * HDIM), lambda at, live: (0, at))
    spatial = pl.pallas_call(
        functools.partial(spatial_kernel, heads),
        out_shape=[pltpu.HBM((patches, columns), LOW)] * 3,
        grid_spec=pltpu.PrefetchScalarGridSpec(
            num_scalar_prefetch=1,
            grid=(SHEADS // heads,),
            in_specs=[block] * 4,
            out_specs=[block] * 3,
        ),
        compiler_params=params(16),
        cost_estimate=pl.CostEstimate(
            flops=10 * SHEADS * patches * patches * HDIM,
            bytes_accessed=14 * patches * SPATIAL,
            transcendentals=SHEADS * patches * patches,
        ),
        name="spatial",
    )(live, *place(pltpu.HBM, *flat))

    half = frame_index % HALVES
    bias_here = lax.dynamic_slice_in_dim(bias, half * HEADS_HERE, HEADS_HERE, 0)
    bias_here = bias_here * LOG2E
    offsets = jnp.concatenate(
        [
            bias_here[:, :frame_count][:, ::-1],
            jnp.full((HEADS_HERE, 1), NEG, WIDE),
            bias_here[:, frame_count:][:, ::-1],
        ],
        axis=1,
    )
    seed = jnp.where(
        jnp.eye(ROWS, dtype=bool)[None, :, None, :], offsets[:, None, :, None], NEG
    ).reshape(HEADS_HERE, ROWS, SPAN)
    gathered, *spatial = lax.optimization_barrier((gathered, *spatial))
    grads, bias_part = pl.pallas_call(
        functools.partial(temporal_kernel, frame_count, heads),
        out_shape=[
            pltpu.HBM((frame_count, 3, ROWS, WIDTH), LOW),
            pltpu.VMEM((HEADS_HERE, ROWS, SPAN), WIDE),
        ],
        in_specs=[spec(pltpu.SMEM), spec(pltpu.VMEM), spec(pltpu.VMEM)],
        out_specs=[spec(pl.ANY), spec(pltpu.VMEM)],
        scratch_shapes=[
            pltpu.VMEM((frame_count, 3, ROWS, WIDTH), LOW),
            pltpu.SemaphoreType.DMA((HEADS_HERE // heads,)),
        ],
        compiler_params=params(16),
        cost_estimate=pl.CostEstimate(
            flops=10 * HEADS_HERE * tokens * tokens * HDIM,
            bytes_accessed=14 * tokens * WIDTH,
            transcendentals=HEADS_HERE * tokens * tokens,
        ),
        name="temporal",
    )(length, *place(pltpu.VMEM, gathered, seed))

    back = lax.all_to_all(grads, "seq", split_axis=0, concat_axis=0, tiled=True)

    sums = jnp.sum(bias_part.reshape(HEADS_HERE, ROWS, SPAN // ROWS, ROWS), axis=(1, 3))
    sums = jnp.concatenate(
        [sums[:, :frame_count][:, ::-1], sums[:, frame_count + 1 :][:, ::-1]], axis=1
    ) / jnp.sqrt(WIDE(lax.axis_size("dp") * frame_count * patches))
    sums = lax.dynamic_update_slice_in_dim(
        jnp.zeros((THEADS, 2 * frame_count - 1), WIDE), sums, half * HEADS_HERE, 0
    )
    for axis, steps in (("dp", (1,)), ("dp", (2, 4, 6)), ("seq", (1, 2, 3)), ("seq", (4, 8, 12))):
        sums = exchange_sum(sums, axis, steps)
    back, sums = lax.optimization_barrier((back, sums))
    bias_grad = exchange_sum(sums, "seq", (16,))

    outputs = pl.pallas_call(
        unpack_kernel,
        out_shape=[pltpu.HBM((groups, ROWS, columns), LOW)] * 3,
        in_specs=[spec(pl.ANY)] * 4,
        out_specs=[spec(pl.ANY)] * 3,
        scratch_shapes=[pltpu.SemaphoreType.DMA((3 * HALVES,))],
        input_output_aliases={1: 0, 2: 1, 3: 2},
        compiler_params=params(8),
        cost_estimate=pl.CostEstimate(
            flops=0, bytes_accessed=12 * patches * SPATIAL, transcendentals=0
        ),
        name="unpack",
    )(
        back.reshape(groups, HALVES, 3, ROWS, WIDTH),
        *place(pltpu.HBM, *(tensor.reshape(groups, ROWS, columns) for tensor in spatial)),
    )
    shaped = tuple(tensor.reshape(1, 1, patches, columns) for tensor in outputs)
    return (*shaped, bias_grad)


def solution(mesh):
    split = P("dp", "seq", None, None)
    return jax.shard_map(
        local,
        mesh=mesh,
        in_specs=(split, split, split, split, P(), P()),
        out_specs=(split, split, split, P()),
        check_vma=False,
    )
```

time: 173 us -> 166 us (0.960)
  Pallas kernels: 26.9 us -> 21.7 us
  local copies, waits for them, and re-layouts: 7.46 us -> 2.8 us
  starting transfers between devices: 32.3 us -> 34.3 us
    ppermute x8 -> x11, waiting for transfers between devices: 50.3 us -> 43.1 us  [exchange_sum(): lax.ppermute(value, axis, [(at, at ^ step) for at in range(count)])]
    all_to_all x1, waiting for transfers between devices: 52.3 us -> 58.9 us  [local(): lax.all_to_all(packed.reshape(frame_count, 4, ROWS, WIDTH), 'seq', split_...]
    pallas_call x5 -> x4, Pallas kernels: 26.9 us -> 21.7 us  [the longest x1 9.21 us: local(): pl.pallas_call(functools.partial(spatial_kernel, heads), out_shape=[pltpu...]
    unnamed x14 -> x6, local copies, waits for them, and re-layouts: 4.55 us -> 0.02 us
    ppermute x8 -> x11, starting transfers between devices: 13.2 us -> 15.2 us  [exchange_sum(): lax.ppermute(value, axis, [(at, at ^ step) for at in range(count)])]
    all_to_all x1, waiting for transfers between devices: 0.01 us -> 1.83 us  [local(): back = lax.all_to_all(grads, 'seq', split_axis=0, concat_axis=0, tiled=True)]
  transfers between devices with their start and end apart: 10 -> 13, of which waited for: 9 -> 9; matrix products, arithmetic and copies ran while one was open for 3% -> 2% of each run, Pallas kernels for 7% -> 6%
where the time goes in v2:
time: 166 us; the launch traced here: 165 us
  waiting for transfers between devices  104 us (63%)
  starting transfers between devices  34.3 us (21%)
  Pallas kernels  21.7 us (13%)
  local copies, waits for them, and re-layouts  2.8 us (2%)
    all_to_all x1, waiting for transfers between devices, local(): lax.all_to_all(packed.reshape(frame_count, 4, ROWS, WIDTH), 'seq', split_...  58.9 us
    ppermute x11, waiting for transfers between devices, exchange_sum(): lax.ppermute(value, axis, [(at, at ^ step) for at in range(count)])  43.1 us
    ppermute x11, starting transfers between devices, exchange_sum(): lax.ppermute(value, axis, [(at, at ^ step) for at in range(count)])  15.2 us
    all_to_all x1, starting transfers between devices, local(): lax.all_to_all(packed.reshape(frame_count, 4, ROWS, WIDTH), 'seq', split_...  11.6 us
    pallas_call x1, Pallas kernels, local(): pl.pallas_call(functools.partial(spatial_kernel, heads), out_shape=[pltpu...  9.21 us
    pallas_call x1, Pallas kernels, local(): pl.pallas_call(functools.partial(temporal_kernel, frame_count, heads), ou...  8.25 us
    all_to_all x1, starting transfers between devices, local(): back = lax.all_to_all(grads, 'seq', split_axis=0, concat_axis=0, tiled=True)  7.49 us
  transfers between devices with their start and end apart: 13, of which 9 were waited for; matrix products, arithmetic and copies ran while one was open for 2% of the time, Pallas kernels for 6%

profile of v2, /device:TPU:4, one launch (start us, length us, event | category | flops | bytes accessed | tf_op | source)
XLA Modules:
  0.0 165.3 jit_solution(5571814060063288243)
XLA Ops:
  0.6 2.8 %pack.1 = bf16[16,2,4,8,1536]{4,3,2,1,0:T(8,128)(2,1)} custom-call(bf16[16,8,6144]{2,1,0:T(8,128)(2,1)} %bitcast.22, bf16[16,8,6144]{2,1,0:T(8,128)(2,1)} %bitcast.24, bf16[16,8,6144]{2,1,0:T(8,128)(2,1)} %bitcast.26, bf16[16,8,6144]{2,1,0:T(8,128)(2,1)} %bitcast.28), custom_call_target="tpu_custom_call" | custom-call | tf_op jit(solution)/shard_map/pack/pallas_call | solution.py:217
  3.5 11.6 %all-to-all-start = ((bf16[32,4,8,1536]{3,2,1,0:T(8,128)(2,1)}), bf16[32,4,8,1536]{3,2,1,0:T(8,128)(2,1)S(1)}, u32[]{:S(2)}, u32[]{:S(2)}) async-start(bf16[32,4,8,1536]{3,2,1,0:T(8,128)(2,1)} %bitcast.21), calls=%async_computation | async-start | bytes 6291456 | tf_op jit(solution)/shard_map/all_to_all | solution.py:230
  15.1 0.6 dynamic_slice.7.length
  16.6 0.2 broadcast_in_dim.34
  17.0 0.2 broadcast_in_dim.36
  17.1 0.8 broadcast_in_dim.37
  18.0 9.2 %spatial.1 = (bf16[128,6144]{1,0:T(8,128)(2,1)}, bf16[128,6144]{1,0:T(8,128)(2,1)}, bf16[128,6144]{1,0:T(8,128)(2,1)}) custom-call(s32[1]{0:T(128)S(6)} %convert_element_type.3.live, bf16[128,6144]{1,0:T(8,128)(2,1)} %bitcast.23, bf16[128,6144]{1,0:T(8,128)(2,1)} %bitcast.25, bf16[128,6144]{1,0:T(8,128)(2,1)} %bitcast.27, bf16[128,6144]{1,0:T(8,128)(2,1)} %bitcast.29), custom_call_target="tpu_custom_call" | custom-call | flops 503316480 | bytes 5505024 | tf_op jit(solution)/shard_map/spatial/pallas_call | solution.py:236
  27.2 58.9 %all-to-all-done.tensors = bf16[32,4,8,1536]{3,2,1,0:T(8,128)(2,1)S(1)} async-done(((bf16[32,4,8,1536]{3,2,1,0:T(8,128)(2,1)}), bf16[32,4,8,1536]{3,2,1,0:T(8,128)(2,1)S(1)}, u32[]{:S(2)}, u32[]{:S(2)}) %all-to-all-start) | async-done | bytes 3145760 | tf_op jit(solution)/shard_map/all_to_all | solution.py:230
  86.2 8.2 %temporal.1 = (bf16[32,3,8,1536]{3,2,1,0:T(8,128)(2,1)}, f32[12,8,512]{2,1,0:T(8,128)S(1)}) custom-call(s32[1]{0:T(128)} %dynamic_slice.7.length, bf16[32,4,8,1536]{3,2,1,0:T(8,128)(2,1)S(1)} %all-to-all-done.tensors, f32[12,8,512]{2,1,0:T(8,128)S(1)} %broadcast_select_fusion.seed), custom_call_target="tpu_custom_call" | custom-call | flops 1006632960 | bytes 5505024 | tf_op jit(solution)/shard_map/temporal/pallas_call | solution.py:269
  94.4 7.5 %all-to-all-start.1 = ((bf16[32,3,8,1536]{3,2,1,0:T(8,128)(2,1)}), bf16[32,3,8,1536]{3,2,1,0:T(8,128)(2,1)S(1)}, u32[]{:S(2)}, u32[]{:S(2)}) async-start(bf16[32,3,8,1536]{3,2,1,0:T(8,128)(2,1)} %get-tuple-element.22), calls=%async_computation.1 | async-start | bytes 4718592 | tf_op jit(solution)/shard_map/all_to_all | solution.py:290
  102.0 0.2 reduce_sum.14
  102.2 0.2 reduce_sum.18
  102.7 0.1 dynamic_update_slice.5
  102.9 1.2 collective-permute-done
  104.3 3.1 %collective-permute-start.3 = (f32[24,63]{1,0:T(8,128)S(1)}, f32[24,63]{1,0:T(8,128)S(1)}, u32[]{:S(2)}, u32[]{:S(2)}) collective-permute-start(f32[24,63]{1,0:T(8,128)S(1)} %add.49), channel_id=1, source_target_pairs={{0,192},{32,224},{64,128},{96,160},{128,64},{160,96},{192,0},{224,... | collective-permute-start | bytes 18152 | tf_op jit(solution)/shard_map/ppermute | solution.py:199
  107.4 0.6 collective-permute-start.2
  108.0 0.4 collective-permute-start.1
  108.5 0.8 collective-permute-done.3
  109.3 3.3 %collective-permute-done.2 = f32[24,63]{1,0:T(8,128)S(1)} collective-permute-done((f32[24,63]{1,0:T(8,128)S(1)}, f32[24,63]{1,0:T(8,128)S(1)}, u32[]{:S(2)}, u32[]{:S(2)}) %collective-permute-start.2) | collective-permute-done | bytes 6080 | tf_op jit(solution)/shard_map/ppermute | solution.py:199
  112.6 0.6 collective-permute-start.6
  113.2 2.7 %collective-permute-start.5 = (f32[24,63]{1,0:T(8,128)S(1)}, f32[24,63]{1,0:T(8,128)S(1)}, u32[]{:S(2)}, u32[]{:S(2)}) collective-permute-start(f32[24,63]{1,0:T(8,128)S(1)} %add_add_fusion.2), channel_id=1, source_target_pairs={{0,2},{1,3},{2,0},{3,1},{4,6},{5,7},{6,4},{7,5},{8,10},{9,11},{10,... | collective-permute-start | bytes 18152 | tf_op jit(solution)/shard_map/ppermute | solution.py:199
  115.9 0.9 collective-permute-start.4
  116.8 1.9 %collective-permute-done.5 = f32[24,63]{1,0:T(8,128)S(1)} collective-permute-done((f32[24,63]{1,0:T(8,128)S(1)}, f32[24,63]{1,0:T(8,128)S(1)}, u32[]{:S(2)}, u32[]{:S(2)}) %collective-permute-start.5) | collective-permute-done | bytes 6080 | tf_op jit(solution)/shard_map/ppermute | solution.py:199
  118.7 1.0 collective-permute-done.4
  119.7 3.3 %collective-permute-start.9 = (f32[24,63]{1,0:T(8,128)S(1)}, f32[24,63]{1,0:T(8,128)S(1)}, u32[]{:S(2)}, u32[]{:S(2)}) collective-permute-start(f32[24,63]{1,0:T(8,128)S(1)} %add_add_fusion.1), channel_id=1, source_target_pairs={{0,12},{1,13},{2,14},{3,15},{4,8},{5,9},{6,10},{7,11},{8,4},{9,5},... | collective-permute-start | bytes 18152 | tf_op jit(solution)/shard_map/ppermute | solution.py:199
  123.0 1.1 collective-permute-start.7
  124.1 31.2 %collective-permute-done.9 = f32[24,63]{1,0:T(8,128)S(1)} collective-permute-done((f32[24,63]{1,0:T(8,128)S(1)}, f32[24,63]{1,0:T(8,128)S(1)}, u32[]{:S(2)}, u32[]{:S(2)}) %collective-permute-start.9) | collective-permute-done | bytes 6080 | tf_op jit(solution)/shard_map/ppermute | solution.py:199
  155.3 1.8 %all-to-all-done.1 = bf16[32,3,8,1536]{3,2,1,0:T(8,128)(2,1)S(1)} async-done(((bf16[32,3,8,1536]{3,2,1,0:T(8,128)(2,1)}), bf16[32,3,8,1536]{3,2,1,0:T(8,128)(2,1)S(1)}, u32[]{:S(2)}, u32[]{:S(2)}) %all-to-all-start.1) | async-done | bytes 2359328 | tf_op jit(solution)/shard_map/all_to_all | solution.py:290
  157.1 2.4 %collective-permute-start.10 = (f32[24,63]{1,0:T(8,128)S(1)}, f32[24,63]{1,0:T(8,128)S(1)}, u32[]{:S(2)}, u32[]{:S(2)}) collective-permute-start(f32[24,63]{1,0:T(8,128)S(1)} %add_add_fusion), channel_id=1, source_target_pairs={{0,16},{1,17},{2,18},{3,19},{4,20},{5,21},{6,22},{7,23},{8,24},{9,... | collective-permute-start | bytes 18152 | tf_op jit(solution)/shard_map/ppermute | solution.py:199
  159.5 1.4 unpack.1
  161.0 3.8 %collective-permute-done.10 = f32[24,63]{1,0:T(8,128)S(1)} collective-permute-done((f32[24,63]{1,0:T(8,128)S(1)}, f32[24,63]{1,0:T(8,128)S(1)}, u32[]{:S(2)}, u32[]{:S(2)}) %collective-permute-start.10) | collective-permute-done | bytes 6080 | tf_op jit(solution)/shard_map/ppermute | solution.py:199
  164.7 0.6 add.59
  (32 shorter events, 1.1 us)
Async XLA Ops:
  3.4 11.6 %copy-start.2 = (s32[8]{0:T(128)S(1)}, s32[8]{0:T(128)}, u32[]{:S(2)}) copy-start(s32[8]{0:T(128)} %param.10) | copy-start | bytes 100
  3.4 12.9 %copy-start.1 = (f32[24,63]{1,0:T(8,128)S(1)}, f32[24,63]{1,0:T(8,128)}, u32[]{:S(2)}) copy-start(f32[24,63]{1,0:T(8,128)} %param.11) | copy-start | bytes 18148
  3.5 82.7 %all-to-all-start = ((bf16[32,4,8,1536]{3,2,1,0:T(8,128)(2,1)}), bf16[32,4,8,1536]{3,2,1,0:T(8,128)(2,1)S(1)}, u32[]{:S(2)}, u32[]{:S(2)}) async-start(bf16[32,4,8,1536]{3,2,1,0:T(8,128)(2,1)} %bitcast.21), calls=%async_computation | async-start | bytes 6291456 | tf_op jit(solution)/shard_map/all_to_all | solution.py:230
  18.0 9.2 %copy-start = (f32[12,512]{1,0:T(8,128)S(1)}, f32[12,512]{1,0:T(8,128)}, u32[]{:S(2)}) copy-start(f32[12,512]{1,0:T(8,128)} %broadcast_in_dim.37) | copy-start | bytes 73732
  94.4 62.7 %all-to-all-start.1 = ((bf16[32,3,8,1536]{3,2,1,0:T(8,128)(2,1)}), bf16[32,3,8,1536]{3,2,1,0:T(8,128)(2,1)S(1)}, u32[]{:S(2)}, u32[]{:S(2)}) async-start(bf16[32,3,8,1536]{3,2,1,0:T(8,128)(2,1)} %get-tuple-element.22), calls=%async_computation.1 | async-start | bytes 4718592 | tf_op jit(solution)/shard_map/all_to_all | solution.py:290
  102.8 1.3 collective-permute-start
  104.3 5.0 %collective-permute-start.3 = (f32[24,63]{1,0:T(8,128)S(1)}, f32[24,63]{1,0:T(8,128)S(1)}, u32[]{:S(2)}, u32[]{:S(2)}) collective-permute-start(f32[24,63]{1,0:T(8,128)S(1)} %add.49), channel_id=1, source_target_pairs={{0,192},{32,224},{64,128},{96,160},{128,64},{160,96},{192,0},{224,... | collective-permute-start | bytes 18152 | tf_op jit(solution)/shard_map/ppermute | solution.py:199
  107.4 5.2 %collective-permute-start.2 = (f32[24,63]{1,0:T(8,128)S(1)}, f32[24,63]{1,0:T(8,128)S(1)}, u32[]{:S(2)}, u32[]{:S(2)}) collective-permute-start(f32[24,63]{1,0:T(8,128)S(1)} %add.49), channel_id=1, source_target_pairs={{0,128},{32,160},{64,192},{96,224},{128,0},{160,32},{192,64},{224,... | collective-permute-start | bytes 18152 | tf_op jit(solution)/shard_map/ppermute | solution.py:199
  108.0 4.6 %collective-permute-start.1 = (f32[24,63]{1,0:T(8,128)S(1)}, f32[24,63]{1,0:T(8,128)S(1)}, u32[]{:S(2)}, u32[]{:S(2)}) collective-permute-start(f32[24,63]{1,0:T(8,128)S(1)} %add.49), channel_id=1, source_target_pairs={{0,64},{32,96},{64,0},{96,32},{128,192},{160,224},{192,128},{224,1... | collective-permute-start | bytes 18152 | tf_op jit(solution)/shard_map/ppermute | solution.py:199
  112.6 4.2 %collective-permute-start.6 = (f32[24,63]{1,0:T(8,128)S(1)}, f32[24,63]{1,0:T(8,128)S(1)}, u32[]{:S(2)}, u32[]{:S(2)}) collective-permute-start(f32[24,63]{1,0:T(8,128)S(1)} %add_add_fusion.2), channel_id=1, source_target_pairs={{0,3},{1,2},{2,1},{3,0},{4,7},{5,6},{6,5},{7,4},{8,11},{9,10},{10,... | collective-permute-start | bytes 18152 | tf_op jit(solution)/shard_map/ppermute | solution.py:199
  113.2 5.5 %collective-permute-start.5 = (f32[24,63]{1,0:T(8,128)S(1)}, f32[24,63]{1,0:T(8,128)S(1)}, u32[]{:S(2)}, u32[]{:S(2)}) collective-permute-start(f32[24,63]{1,0:T(8,128)S(1)} %add_add_fusion.2), channel_id=1, source_target_pairs={{0,2},{1,3},{2,0},{3,1},{4,6},{5,7},{6,4},{7,5},{8,10},{9,11},{10,... | collective-permute-start | bytes 18152 | tf_op jit(solution)/shard_map/ppermute | solution.py:199
  115.9 3.8 %collective-permute-start.4 = (f32[24,63]{1,0:T(8,128)S(1)}, f32[24,63]{1,0:T(8,128)S(1)}, u32[]{:S(2)}, u32[]{:S(2)}) collective-permute-start(f32[24,63]{1,0:T(8,128)S(1)} %add_add_fusion.2), channel_id=1, source_target_pairs={{0,1},{1,0},{2,3},{3,2},{4,5},{5,4},{6,7},{7,6},{8,9},{9,8},{10,11... | collective-permute-start | bytes 18152 | tf_op jit(solution)/shard_map/ppermute | solution.py:199
  119.7 35.6 %collective-permute-start.9 = (f32[24,63]{1,0:T(8,128)S(1)}, f32[24,63]{1,0:T(8,128)S(1)}, u32[]{:S(2)}, u32[]{:S(2)}) collective-permute-start(f32[24,63]{1,0:T(8,128)S(1)} %add_add_fusion.1), channel_id=1, source_target_pairs={{0,12},{1,13},{2,14},{3,15},{4,8},{5,9},{6,10},{7,11},{8,4},{9,5},... | collective-permute-start | bytes 18152 | tf_op jit(solution)/shard_map/ppermute | solution.py:199
  123.0 32.3 %collective-permute-start.8 = (f32[24,63]{1,0:T(8,128)S(1)}, f32[24,63]{1,0:T(8,128)S(1)}, u32[]{:S(2)}, u32[]{:S(2)}) collective-permute-start(f32[24,63]{1,0:T(8,128)S(1)} %add_add_fusion.1), channel_id=1, source_target_pairs={{0,8},{1,9},{2,10},{3,11},{4,12},{5,13},{6,14},{7,15},{8,0},{9,1},... | collective-permute-start | bytes 18152 | tf_op jit(solution)/shard_map/ppermute | solution.py:199
  123.0 32.3 %collective-permute-start.7 = (f32[24,63]{1,0:T(8,128)S(1)}, f32[24,63]{1,0:T(8,128)S(1)}, u32[]{:S(2)}, u32[]{:S(2)}) collective-permute-start(f32[24,63]{1,0:T(8,128)S(1)} %add_add_fusion.1), channel_id=1, source_target_pairs={{0,4},{1,5},{2,6},{3,7},{4,0},{5,1},{6,2},{7,3},{8,12},{9,13},{10,... | collective-permute-start | bytes 18152 | tf_op jit(solution)/shard_map/ppermute | solution.py:199
  157.1 7.6 %collective-permute-start.10 = (f32[24,63]{1,0:T(8,128)S(1)}, f32[24,63]{1,0:T(8,128)S(1)}, u32[]{:S(2)}, u32[]{:S(2)}) collective-permute-start(f32[24,63]{1,0:T(8,128)S(1)} %add_add_fusion), channel_id=1, source_target_pairs={{0,16},{1,17},{2,18},{3,19},{4,20},{5,21},{6,22},{7,23},{8,24},{9,... | collective-permute-start | bytes 18152 | tf_op jit(solution)/shard_map/ppermute | solution.py:199

commit v3 on v2

--- a/solution.py
+++ b/solution.py
@@ -32,20 +32,25 @@
     return lax.dot_general(left, right, dims, preferred_element_type=WIDE)
 
 
-def head_grads(query, keys, values, grad, extra):
-    logits = dot(keys, query, NT) * (SCALE * LOG2E)
+def products(query, keys, values, grad):
+    return dot(keys, query, NT), dot(values, grad, NT)
+
+
+def soften(logits, grad_attention, extra):
+    logits = logits * (SCALE * LOG2E)
     if extra is not None:
         logits = logits + extra
     exponent = jnp.exp2(logits - jnp.max(logits, axis=0, keepdims=True))
     attention = exponent * (1.0 / jnp.sum(exponent, axis=0, keepdims=True))
-    grad_attention = dot(values, grad, NT)
     row_delta = jnp.sum(attention * grad_attention, axis=0, keepdims=True)
-    grad_logits = attention * (grad_attention - row_delta)
-    grad_low = grad_logits.astype(LOW)
+    return attention.astype(LOW), attention * (grad_attention - row_delta)
+
+
+def token_grads(attention_low, grad_low, query, keys, grad):
     grad_query = (dot(grad_low, keys, TN) * SCALE).astype(LOW)
     grad_keys = (dot(grad_low, query, NN) * SCALE).astype(LOW)
-    grad_values = dot(attention.astype(LOW), grad, NN).astype(LOW)
-    return grad_query, grad_keys, grad_values, grad_logits
+    grad_values = dot(attention_low, grad, NN).astype(LOW)
+    return grad_query, grad_keys, grad_values
 
 
 def pack_kernel(query, keys, values, grad, packed, staged, in_sems, out_sems):
@@ -95,8 +100,10 @@
     flag = live[0].astype(WIDE).astype(LOW)
     for head in range(heads):
         cols = pl.ds(head * HDIM, HDIM)
-        outs = head_grads(
-            query[:, cols], keys[:, cols], values[:, cols], grad[:, cols] * flag, None
+        tokens = query[:, cols], keys[:, cols], values[:, cols], grad[:, cols] * flag
+        attention_low, grad_logits = soften(*products(*tokens), None)
+        outs = token_grads(
+            attention_low, grad_logits.astype(LOW), tokens[0], tokens[1], tokens[3]
         )
         grad_query[:, cols] = outs[0]
         grad_keys[:, cols] = outs[1]
@@ -142,43 +149,56 @@
     return parts[0]
 
 
-def temporal_kernel(
-    frame_count, heads, length, tensors, seed, grads, bias_part, staged, sems
-):
+def temporal_kernel(frame_count, length, tensors, seed, grads, grad_logits, staged, kept, sems):
     tokens = frame_count * ROWS
     live_rows = lax.broadcasted_iota(jnp.int32, (tokens, HDIM), 0) < length[0] * ROWS
-
-    def one_head(head):
-        cols = pl.ds(pl.multiple_of(head * HDIM, HDIM), HDIM)
+    copies = []
+
+    def load(head):
+        cols = pl.ds(head * HDIM, HDIM)
         query, keys, values, grad = (
             tensors[:, number, :, cols].reshape(tokens, HDIM) for number in range(4)
         )
-        grad = jnp.where(live_rows, grad.astype(WIDE), 0.0).astype(LOW)
+        return query, keys, values, jnp.where(live_rows, grad.astype(WIDE), 0.0).astype(LOW)
+
+    def send(source, target, at):
+        copy = pltpu.make_async_copy(source, target, sems.at[at])
+        copy.start()
+        copies.append(copy)
+
+    def finish(head, held, attention_low, grad_low):
+        outs = token_grads(attention_low, grad_low, held[0], held[1], held[3])
+        for number in range(3):
+            staged[:, number, :, pl.ds(head * HDIM, HDIM)] = outs[number].reshape(
+                frame_count, ROWS, HDIM
+            )
+        if head % 2:
+            cols = pl.ds((head - 1) * HDIM, 2 * HDIM)
+            send(staged.at[:, :, :, cols], grads.at[:, :, :, cols], HEADS_HERE + head // 2)
+
+    held = load(0)
+    ready = products(*held)
+    waiting = None
+    for head in range(HEADS_HERE):
+        held_next = ready_next = None
+        if head + 1 < HEADS_HERE:
+            held_next = load(head + 1)
+            ready_next = products(*held_next)
         table = moved_rows(seed[head], frame_count, length[0])
-        outs = head_grads(query, keys, values, grad, table)
-        for number in range(3):
-            staged[:, number, :, cols] = outs[number].reshape(frame_count, ROWS, HDIM)
-        terms = outs[3].reshape(frame_count, ROWS, tokens)
-        bias_part[head] = offset_sums(terms, frame_count)
-
-    def write(at):
-        cols = pl.ds(pl.multiple_of(at * heads * HDIM, HDIM), heads * HDIM)
-        return pltpu.make_async_copy(
-            staged.at[:, :, :, cols], grads.at[:, :, :, cols], sems.at[at]
-        )
-
-    def step(at, carry):
-        for offset in range(heads):
-            one_head(at * heads + offset)
-        write(at).start()
-        return carry
-
-    def finish(at, carry):
-        write(at).wait()
-        return carry
-
-    lax.fori_loop(0, HEADS_HERE // heads, step, 0)
-    lax.fori_loop(0, HEADS_HERE // heads, finish, 0)
+        attention_low, logits_grad = soften(*ready, table)
+        kept[head] = logits_grad
+        send(kept.at[head], grad_logits.at[head], head)
+        if waiting is not None:
+            finish(*waiting)
+        waiting = head, held, attention_low, logits_grad.astype(LOW)
+        held, ready = held_next, ready_next
+    finish(*waiting)
+    for copy in copies:
+        copy.wait()
+
+
+def bias_kernel(frame_count, terms, sums):
+    sums[0] = offset_sums(terms[0].reshape(frame_count, ROWS, -1), frame_count)
 
 
 def spec(space):
@@ -193,14 +213,31 @@
     return pltpu.CompilerParams(vmem_limit_bytes=limit * MIB)
 
 
-def exchange_sum(value, axis, steps):
-    count = lax.axis_size(axis)
-    pieces = [value] + [
-        lax.ppermute(value, axis, [(at, at ^ step) for at in range(count)]) for step in steps
-    ]
+def tree_sum(pieces):
     while len(pieces) > 1:
         pieces = [pieces[at] + pieces[at + 1] for at in range(0, len(pieces), 2)]
     return pieces[0]
+
+
+def exchange_sum(value, axis, steps):
+    count = lax.axis_size(axis)
+    return tree_sum(
+        [value]
+        + [lax.ppermute(value, axis, [(at, at ^ step) for at in range(count)]) for step in steps]
+    )
+
+
+def split_sum(value, low_steps, high_steps):
+    clips, count = lax.axis_size("dp"), lax.axis_size("seq")
+    pieces = []
+    for steps in zip(low_steps, high_steps):
+        pairs = [
+            (clip * count + at, clip * count + (at ^ steps[clip % 2]))
+            for clip in range(clips)
+            for at in range(count)
+        ]
+        pieces.append(lax.ppermute(value, ("dp", "seq"), pairs))
+    return tree_sum(pieces)
 
 
 def local(query, keys, values, grad_out, frames, bias):
@@ -266,19 +303,20 @@
         jnp.eye(ROWS, dtype=bool)[None, :, None, :], offsets[:, None, :, None], NEG
     ).reshape(HEADS_HERE, ROWS, SPAN)
     gathered, *spatial = lax.optimization_barrier((gathered, *spatial))
-    grads, bias_part = pl.pallas_call(
-        functools.partial(temporal_kernel, frame_count, heads),
+    grads, grad_logits = pl.pallas_call(
+        functools.partial(temporal_kernel, frame_count),
         out_shape=[
             pltpu.HBM((frame_count, 3, ROWS, WIDTH), LOW),
-            pltpu.VMEM((HEADS_HERE, ROWS, SPAN), WIDE),
+            pltpu.HBM((HEADS_HERE, tokens, tokens), WIDE),
         ],
         in_specs=[spec(pltpu.SMEM), spec(pltpu.VMEM), spec(pltpu.VMEM)],
-        out_specs=[spec(pl.ANY), spec(pltpu.VMEM)],
+        out_specs=[spec(pl.ANY)] * 2,
         scratch_shapes=[
             pltpu.VMEM((frame_count, 3, ROWS, WIDTH), LOW),
-            pltpu.SemaphoreType.DMA((HEADS_HERE // heads,)),
+            pltpu.VMEM((HEADS_HERE, tokens, tokens), WIDE),
+            pltpu.SemaphoreType.DMA((HEADS_HERE + HEADS_HERE // 2,)),
         ],
-        compiler_params=params(16),
+        compiler_params=params(24),
         cost_estimate=pl.CostEstimate(
             flops=10 * HEADS_HERE * tokens * tokens * HDIM,
             bytes_accessed=14 * tokens * WIDTH,
@@ -286,6 +324,20 @@
         ),
         name="temporal",
     )(length, *place(pltpu.VMEM, gathered, seed))
+    bias_part = pl.pallas_call(
+        functools.partial(bias_kernel, frame_count),
+        out_shape=jax.ShapeDtypeStruct((HEADS_HERE, ROWS, SPAN), WIDE),
+        grid=(HEADS_HERE,),
+        in_specs=[pl.BlockSpec((1, tokens, tokens), lambda at: (at, 0, 0))],
+        out_specs=pl.BlockSpec((1, ROWS, SPAN), lambda at: (at, 0, 0)),
+        compiler_params=params(8),
+        cost_estimate=pl.CostEstimate(
+            flops=4 * HEADS_HERE * tokens * tokens,
+            bytes_accessed=4 * HEADS_HERE * tokens * tokens,
+            transcendentals=0,
+        ),
+        name="offsets",
+    )(*place(pltpu.HBM, grad_logits))
 
     back = lax.all_to_all(grads, "seq", split_axis=0, concat_axis=0, tiled=True)
 
@@ -296,10 +348,11 @@
     sums = lax.dynamic_update_slice_in_dim(
         jnp.zeros((THEADS, 2 * frame_count - 1), WIDE), sums, half * HEADS_HERE, 0
     )
-    for axis, steps in (("dp", (1,)), ("dp", (2, 4, 6)), ("seq", (1, 2, 3)), ("seq", (4, 8, 12))):
+    for axis, steps in (("dp", (1,)), ("dp", (2, 4, 6)), ("seq", (1, 2, 3))):
         sums = exchange_sum(sums, axis, steps)
+    sums = split_sum(sums, (0, 4, 8, 12), (16, 20, 24, 28))
     back, sums = lax.optimization_barrier((back, sums))
-    bias_grad = exchange_sum(sums, "seq", (16,))
+    bias_grad = exchange_sum(sums, "dp", (1,))
 
     outputs = pl.pallas_call(
         unpack_kernel,

time: 166 us -> 158 us (0.952)
  waiting for transfers between devices: 104 us -> 92.2 us
  Pallas kernels: 21.7 us -> 26.4 us
    ppermute x11 -> x8, waiting for transfers between devices: 43.1 us -> 8.95 us  [exchange_sum(): lax.ppermute(value, axis, [(at, at ^ step) for at in range(count)])]
    ppermute x0 -> x4, waiting for transfers between devices: none -> 21.5 us  [split_sum(): pieces.append(lax.ppermute(value, ('dp', 'seq'), pairs))]
    ppermute x11 -> x8, starting transfers between devices: 15.2 us -> 8.37 us  [exchange_sum(): lax.ppermute(value, axis, [(at, at ^ step) for at in range(count)])]
    ppermute x0 -> x4, starting transfers between devices: none -> 5.2 us  [split_sum(): pieces.append(lax.ppermute(value, ('dp', 'seq'), pairs))]
    pallas_call x1 -> x2, Pallas kernels: 8.25 us -> 12.9 us  [the longest x1 7.77 us: local(): pl.pallas_call(functools.partial(bias_kernel, frame_count), out_shape=jax...]
  transfers between devices with their start and end apart: 13 -> 14, of which waited for: 9 -> 9; matrix products, arithmetic and copies ran while one was open for 2% -> 2% of each run, Pallas kernels for 6% -> 12%
where the time goes in v3:
time: 158 us; the launch traced here: 157 us
  waiting for transfers between devices  92.2 us (58%)
  starting transfers between devices  32.7 us (21%)
  Pallas kernels  26.4 us (17%)
  local copies, waits for them, and re-layouts  2.81 us (2%)
    all_to_all x1, waiting for transfers between devices, local(): lax.all_to_all(packed.reshape(frame_count, 4, ROWS, WIDTH), 'seq', split_...  58.9 us
    ppermute x4, waiting for transfers between devices, split_sum(): pieces.append(lax.ppermute(value, ('dp', 'seq'), pairs))  21.5 us
    all_to_all x1, starting transfers between devices, local(): lax.all_to_all(packed.reshape(frame_count, 4, ROWS, WIDTH), 'seq', split_...  11.6 us
    pallas_call x1, Pallas kernels, local(): pl.pallas_call(functools.partial(spatial_kernel, heads), out_shape=[pltpu...  9.22 us
    ppermute x8, waiting for transfers between devices, exchange_sum(): lax.ppermute(value, axis, [(at, at ^ step) for at in range(count)])  8.95 us
    ppermute x8, starting transfers between devices, exchange_sum(): lax.ppermute(value, axis, [(at, at ^ step) for at in range(count)])  8.37 us
    pallas_call x1, Pallas kernels, local(): pl.pallas_call(functools.partial(bias_kernel, frame_count), out_shape=jax...  7.77 us
    all_to_all x1, starting transfers between devices, local(): back = lax.all_to_all(grads, 'seq', split_axis=0, concat_axis=0, tiled=True)  7.5 us
  transfers between devices with their start and end apart: 14, of which 9 were waited for; matrix products, arithmetic and copies ran while one was open for 2% of the time, Pallas kernels for 12%

profile of v3, /device:TPU:4, one launch (start us, length us, event | category | flops | bytes accessed | tf_op | source)
XLA Modules:
  0.0 156.7 jit_solution(11859428718253872236)
XLA Ops:
  0.6 2.8 %pack.1 = bf16[16,2,4,8,1536]{4,3,2,1,0:T(8,128)(2,1)} custom-call(bf16[16,8,6144]{2,1,0:T(8,128)(2,1)} %bitcast.22, bf16[16,8,6144]{2,1,0:T(8,128)(2,1)} %bitcast.24, bf16[16,8,6144]{2,1,0:T(8,128)(2,1)} %bitcast.26, bf16[16,8,6144]{2,1,0:T(8,128)(2,1)} %bitcast.28), custom_call_target="tpu_custom_call" | custom-call | tf_op jit(solution)/shard_map/pack/pallas_call | solution.py:254
  3.5 11.6 %all-to-all-start = ((bf16[32,4,8,1536]{3,2,1,0:T(8,128)(2,1)}), bf16[32,4,8,1536]{3,2,1,0:T(8,128)(2,1)S(1)}, u32[]{:S(2)}, u32[]{:S(2)}) async-start(bf16[32,4,8,1536]{3,2,1,0:T(8,128)(2,1)} %bitcast.21), calls=%async_computation | async-start | bytes 6291456 | tf_op jit(solution)/shard_map/all_to_all | solution.py:267
  15.5 0.2 broadcast_in_dim.36
  15.7 0.8 broadcast_in_dim.37
  16.6 0.2 broadcast_in_dim.34
  16.8 0.6 dynamic_slice.7.length
  18.0 9.2 %spatial.1 = (bf16[128,6144]{1,0:T(8,128)(2,1)}, bf16[128,6144]{1,0:T(8,128)(2,1)}, bf16[128,6144]{1,0:T(8,128)(2,1)}) custom-call(s32[1]{0:T(128)S(6)} %convert_element_type.3.live, bf16[128,6144]{1,0:T(8,128)(2,1)} %bitcast.23, bf16[128,6144]{1,0:T(8,128)(2,1)} %bitcast.25, bf16[128,6144]{1,0:T(8,128)(2,1)} %bitcast.27, bf16[128,6144]{1,0:T(8,128)(2,1)} %bitcast.29), custom_call_target="tpu_custom_call" | custom-call | flops 503316480 | bytes 5505024 | tf_op jit(solution)/shard_map/spatial/pallas_call | solution.py:273
  27.3 58.9 %all-to-all-done.tensors = bf16[32,4,8,1536]{3,2,1,0:T(8,128)(2,1)S(1)} async-done(((bf16[32,4,8,1536]{3,2,1,0:T(8,128)(2,1)}), bf16[32,4,8,1536]{3,2,1,0:T(8,128)(2,1)S(1)}, u32[]{:S(2)}, u32[]{:S(2)}) %all-to-all-start) | async-done | bytes 3145760 | tf_op jit(solution)/shard_map/all_to_all | solution.py:267
  86.2 5.1 %temporal.1 = (bf16[32,3,8,1536]{3,2,1,0:T(8,128)(2,1)}, f32[12,256,256]{2,1,0:T(8,128)}) custom-call(s32[1]{0:T(128)} %dynamic_slice.7.length, bf16[32,4,8,1536]{3,2,1,0:T(8,128)(2,1)S(1)} %all-to-all-done.tensors, f32[12,8,512]{2,1,0:T(8,128)S(1)} %broadcast_select_fusion.seed), custom_call_target="tpu_custom_call" | custom-call | flops 1006632960 | bytes 5505024 | tf_op jit(solution)/shard_map/temporal/pallas_call | solution.py:306
  91.3 7.5 %all-to-all-start.1 = ((bf16[32,3,8,1536]{3,2,1,0:T(8,128)(2,1)}), bf16[32,3,8,1536]{3,2,1,0:T(8,128)(2,1)S(1)}, u32[]{:S(2)}, u32[]{:S(2)}) async-start(bf16[32,3,8,1536]{3,2,1,0:T(8,128)(2,1)} %get-tuple-element.22), calls=%async_computation.1 | async-start | bytes 4718592 | tf_op jit(solution)/shard_map/all_to_all | solution.py:342
  98.9 7.8 %offsets.1 = f32[12,8,512]{2,1,0:T(8,128)S(1)} custom-call(f32[12,256,256]{2,1,0:T(8,128)} %get-tuple-element.23.terms), custom_call_target="tpu_custom_call" | custom-call | flops 3145728 | bytes 3145728 | tf_op jit(solution)/shard_map/offsets/pallas_call | solution.py:327
  106.7 0.2 reduce_sum.14
  106.9 0.2 reduce_sum.18
  107.7 1.2 collective-permute-done
  109.0 1.7 %collective-permute-start.1 = (f32[24,63]{1,0:T(8,128)S(1)}, f32[24,63]{1,0:T(8,128)S(1)}, u32[]{:S(2)}, u32[]{:S(2)}) collective-permute-start(f32[24,63]{1,0:T(8,128)S(1)} %add.49), channel_id=1, source_target_pairs={{0,64},{32,96},{64,0},{96,32},{128,192},{160,224},{192,128},{224,1... | collective-permute-start | bytes 18152 | tf_op jit(solution)/shard_map/ppermute | solution.py:226
  110.7 2.9 %collective-permute-start.2 = (f32[24,63]{1,0:T(8,128)S(1)}, f32[24,63]{1,0:T(8,128)S(1)}, u32[]{:S(2)}, u32[]{:S(2)}) collective-permute-start(f32[24,63]{1,0:T(8,128)S(1)} %add.49), channel_id=1, source_target_pairs={{0,128},{32,160},{64,192},{96,224},{128,0},{160,32},{192,64},{224,... | collective-permute-start | bytes 18152 | tf_op jit(solution)/shard_map/ppermute | solution.py:226
  113.6 0.2 collective-permute-start.3
  113.8 2.1 %collective-permute-done.2 = f32[24,63]{1,0:T(8,128)S(1)} collective-permute-done((f32[24,63]{1,0:T(8,128)S(1)}, f32[24,63]{1,0:T(8,128)S(1)}, u32[]{:S(2)}, u32[]{:S(2)}) %collective-permute-start.2) | collective-permute-done | bytes 6080 | tf_op jit(solution)/shard_map/ppermute | solution.py:226
  115.9 2.6 %collective-permute-done.3 = f32[24,63]{1,0:T(8,128)S(1)} collective-permute-done((f32[24,63]{1,0:T(8,128)S(1)}, f32[24,63]{1,0:T(8,128)S(1)}, u32[]{:S(2)}, u32[]{:S(2)}) %collective-permute-start.3) | collective-permute-done | bytes 6080 | tf_op jit(solution)/shard_map/ppermute | solution.py:226
  118.5 1.1 collective-permute-start.4
  119.6 0.9 collective-permute-start.5
  120.5 1.5 collective-permute-start.6
  122.0 0.2 collective-permute-done.4
  122.2 2.9 %collective-permute-done.5 = f32[24,63]{1,0:T(8,128)S(1)} collective-permute-done((f32[24,63]{1,0:T(8,128)S(1)}, f32[24,63]{1,0:T(8,128)S(1)}, u32[]{:S(2)}, u32[]{:S(2)}) %collective-permute-start.5) | collective-permute-done | bytes 6080 | tf_op jit(solution)/shard_map/ppermute | solution.py:226
  125.1 3.2 %collective-permute-start.10 = (f32[24,63]{1,0:T(8,128)S(1)}, f32[24,63]{1,0:T(8,128)S(1)}, u32[]{:S(2)}, u32[]{:S(2)}) collective-permute-start(f32[24,63]{1,0:T(8,128)S(1)} %add_add_fusion.1), channel_id=1, source_target_pairs={{0,12},{1,13},{2,14},{3,15},{4,8},{5,9},{6,10},{7,11},{8,4},{9,5},... | collective-permute-start | bytes 18152 | tf_op jit(solution)/shard_map/ppermute | solution.py:239
  128.3 0.7 collective-permute-start.7
  129.1 1.2 collective-permute-start.9
  130.3 20.2 %collective-permute-done.10 = f32[24,63]{1,0:T(8,128)S(1)} collective-permute-done((f32[24,63]{1,0:T(8,128)S(1)}, f32[24,63]{1,0:T(8,128)S(1)}, u32[]{:S(2)}, u32[]{:S(2)}) %collective-permute-start.10) | collective-permute-done | bytes 6080 | tf_op jit(solution)/shard_map/ppermute | solution.py:239
  150.5 1.3 collective-permute-done.8
  151.8 2.8 %all-to-all-done.1 = bf16[32,3,8,1536]{3,2,1,0:T(8,128)(2,1)S(1)} async-done(((bf16[32,3,8,1536]{3,2,1,0:T(8,128)(2,1)}), bf16[32,3,8,1536]{3,2,1,0:T(8,128)(2,1)S(1)}, u32[]{:S(2)}, u32[]{:S(2)}) %all-to-all-start.1) | async-done | bytes 2359328 | tf_op jit(solution)/shard_map/all_to_all | solution.py:342
  154.6 1.4 unpack.1
  156.1 0.6 add.59
  (35 shorter events, 1.4 us)
Async XLA Ops:
  3.5 11.7 %copy-start.1 = (f32[24,63]{1,0:T(8,128)S(1)}, f32[24,63]{1,0:T(8,128)}, u32[]{:S(2)}) copy-start(f32[24,63]{1,0:T(8,128)} %param.11) | copy-start | bytes 18148
  3.5 13.3 %copy-start.2 = (s32[8]{0:T(128)S(1)}, s32[8]{0:T(128)}, u32[]{:S(2)}) copy-start(s32[8]{0:T(128)} %param.10) | copy-start | bytes 100
  3.5 82.7 %all-to-all-start = ((bf16[32,4,8,1536]{3,2,1,0:T(8,128)(2,1)}), bf16[32,4,8,1536]{3,2,1,0:T(8,128)(2,1)S(1)}, u32[]{:S(2)}, u32[]{:S(2)}) async-start(bf16[32,4,8,1536]{3,2,1,0:T(8,128)(2,1)} %bitcast.21), calls=%async_computation | async-start | bytes 6291456 | tf_op jit(solution)/shard_map/all_to_all | solution.py:267
  18.0 9.2 %copy-start = (f32[12,512]{1,0:T(8,128)S(1)}, f32[12,512]{1,0:T(8,128)}, u32[]{:S(2)}) copy-start(f32[12,512]{1,0:T(8,128)} %broadcast_in_dim.37) | copy-start | bytes 73732
  91.3 63.3 %all-to-all-start.1 = ((bf16[32,3,8,1536]{3,2,1,0:T(8,128)(2,1)}), bf16[32,3,8,1536]{3,2,1,0:T(8,128)(2,1)S(1)}, u32[]{:S(2)}, u32[]{:S(2)}) async-start(bf16[32,3,8,1536]{3,2,1,0:T(8,128)(2,1)} %get-tuple-element.22), calls=%async_computation.1 | async-start | bytes 4718592 | tf_op jit(solution)/shard_map/all_to_all | solution.py:342
  107.5 1.3 collective-permute-start
  109.0 4.8 %collective-permute-start.1 = (f32[24,63]{1,0:T(8,128)S(1)}, f32[24,63]{1,0:T(8,128)S(1)}, u32[]{:S(2)}, u32[]{:S(2)}) collective-permute-start(f32[24,63]{1,0:T(8,128)S(1)} %add.49), channel_id=1, source_target_pairs={{0,64},{32,96},{64,0},{96,32},{128,192},{160,224},{192,128},{224,1... | collective-permute-start | bytes 18152 | tf_op jit(solution)/shard_map/ppermute | solution.py:226
  110.7 5.2 %collective-permute-start.2 = (f32[24,63]{1,0:T(8,128)S(1)}, f32[24,63]{1,0:T(8,128)S(1)}, u32[]{:S(2)}, u32[]{:S(2)}) collective-permute-start(f32[24,63]{1,0:T(8,128)S(1)} %add.49), channel_id=1, source_target_pairs={{0,128},{32,160},{64,192},{96,224},{128,0},{160,32},{192,64},{224,... | collective-permute-start | bytes 18152 | tf_op jit(solution)/shard_map/ppermute | solution.py:226
  113.6 4.9 %collective-permute-start.3 = (f32[24,63]{1,0:T(8,128)S(1)}, f32[24,63]{1,0:T(8,128)S(1)}, u32[]{:S(2)}, u32[]{:S(2)}) collective-permute-start(f32[24,63]{1,0:T(8,128)S(1)} %add.49), channel_id=1, source_target_pairs={{0,192},{32,224},{64,128},{96,160},{128,64},{160,96},{192,0},{224,... | collective-permute-start | bytes 18152 | tf_op jit(solution)/shard_map/ppermute | solution.py:226
  118.5 3.7 %collective-permute-start.4 = (f32[24,63]{1,0:T(8,128)S(1)}, f32[24,63]{1,0:T(8,128)S(1)}, u32[]{:S(2)}, u32[]{:S(2)}) collective-permute-start(f32[24,63]{1,0:T(8,128)S(1)} %add_add_fusion.2), channel_id=1, source_target_pairs={{0,1},{1,0},{2,3},{3,2},{4,5},{5,4},{6,7},{7,6},{8,9},{9,8},{10,11... | collective-permute-start | bytes 18152 | tf_op jit(solution)/shard_map/ppermute | solution.py:226
  119.6 5.4 %collective-permute-start.5 = (f32[24,63]{1,0:T(8,128)S(1)}, f32[24,63]{1,0:T(8,128)S(1)}, u32[]{:S(2)}, u32[]{:S(2)}) collective-permute-start(f32[24,63]{1,0:T(8,128)S(1)} %add_add_fusion.2), channel_id=1, source_target_pairs={{0,2},{1,3},{2,0},{3,1},{4,6},{5,7},{6,4},{7,5},{8,10},{9,11},{10,... | collective-permute-start | bytes 18152 | tf_op jit(solution)/shard_map/ppermute | solution.py:226
  120.5 4.6 %collective-permute-start.6 = (f32[24,63]{1,0:T(8,128)S(1)}, f32[24,63]{1,0:T(8,128)S(1)}, u32[]{:S(2)}, u32[]{:S(2)}) collective-permute-start(f32[24,63]{1,0:T(8,128)S(1)} %add_add_fusion.2), channel_id=1, source_target_pairs={{0,3},{1,2},{2,1},{3,0},{4,7},{5,6},{6,5},{7,4},{8,11},{9,10},{10,... | collective-permute-start | bytes 18152 | tf_op jit(solution)/shard_map/ppermute | solution.py:226
  125.1 25.5 %collective-permute-start.10 = (f32[24,63]{1,0:T(8,128)S(1)}, f32[24,63]{1,0:T(8,128)S(1)}, u32[]{:S(2)}, u32[]{:S(2)}) collective-permute-start(f32[24,63]{1,0:T(8,128)S(1)} %add_add_fusion.1), channel_id=1, source_target_pairs={{0,12},{1,13},{2,14},{3,15},{4,8},{5,9},{6,10},{7,11},{8,4},{9,5},... | collective-permute-start | bytes 18152 | tf_op jit(solution)/shard_map/ppermute | solution.py:239
  128.3 22.2 %collective-permute-start.7 = (f32[24,63]{1,0:T(8,128)S(1)}, f32[24,63]{1,0:T(8,128)S(1)}, u32[]{:S(2)}, u32[]{:S(2)}) collective-permute-start(f32[24,63]{1,0:T(8,128)S(1)} %add_add_fusion.1), channel_id=1, source_target_pairs={{0,0},{1,1},{2,2},{3,3},{4,4},{5,5},{6,6},{7,7},{8,8},{9,9},{10,10... | collective-permute-start | bytes 18152 | tf_op jit(solution)/shard_map/ppermute | solution.py:239
  129.0 22.8 %collective-permute-start.8 = (f32[24,63]{1,0:T(8,128)S(1)}, f32[24,63]{1,0:T(8,128)S(1)}, u32[]{:S(2)}, u32[]{:S(2)}) collective-permute-start(f32[24,63]{1,0:T(8,128)S(1)} %add_add_fusion.1), channel_id=1, source_target_pairs={{0,4},{1,5},{2,6},{3,7},{4,0},{5,1},{6,2},{7,3},{8,12},{9,13},{10,... | collective-permute-start | bytes 18152 | tf_op jit(solution)/shard_map/ppermute | solution.py:239
  129.1 22.7 %collective-permute-start.9 = (f32[24,63]{1,0:T(8,128)S(1)}, f32[24,63]{1,0:T(8,128)S(1)}, u32[]{:S(2)}, u32[]{:S(2)}) collective-permute-start(f32[24,63]{1,0:T(8,128)S(1)} %add_add_fusion.1), channel_id=1, source_target_pairs={{0,8},{1,9},{2,10},{3,11},{4,12},{5,13},{6,14},{7,15},{8,0},{9,1},... | collective-permute-start | bytes 18152 | tf_op jit(solution)/shard_map/ppermute | solution.py:239
  154.6 1.5 collective-permute-start.11

commit v4 on v3

--- a/solution.py
+++ b/solution.py
@@ -351,8 +351,9 @@
     for axis, steps in (("dp", (1,)), ("dp", (2, 4, 6)), ("seq", (1, 2, 3))):
         sums = exchange_sum(sums, axis, steps)
     sums = split_sum(sums, (0, 4, 8, 12), (16, 20, 24, 28))
-    back, sums = lax.optimization_barrier((back, sums))
-    bias_grad = exchange_sum(sums, "dp", (1,))
+    other = lax.ppermute(
+        sums, "dp", [(clip, clip ^ 1) for clip in range(lax.axis_size("dp"))]
+    )
 
     outputs = pl.pallas_call(
         unpack_kernel,
@@ -370,6 +371,8 @@
         back.reshape(groups, HALVES, 3, ROWS, WIDTH),
         *place(pltpu.HBM, *(tensor.reshape(groups, ROWS, columns) for tensor in spatial)),
     )
+    *outputs, other = lax.optimization_barrier((*outputs, other))
+    bias_grad = sums + other
     shaped = tuple(tensor.reshape(1, 1, patches, columns) for tensor in outputs)
     return (*shaped, bias_grad)
 

time: 158 us -> 158 us (level)
  waiting for transfers between devices: 92.2 us -> 89.4 us
  starting transfers between devices: 32.7 us -> 35.4 us
    all_to_all x1, waiting for transfers between devices: 2.8 us -> 0.08 us  [local(): back = lax.all_to_all(grads, 'seq', split_axis=0, concat_axis=0, tiled=True)]
    ppermute x0 -> x1, starting transfers between devices: none -> 2.71 us  [local(): lax.ppermute(sums, 'dp', [(clip, clip ^ 1) for clip in range(lax.axis_siz...]
    ppermute x8 -> x7, starting transfers between devices: 8.37 us -> 8.37 us  [exchange_sum(): lax.ppermute(value, axis, [(at, at ^ step) for at in range(count)])]
    ppermute x8 -> x7, waiting for transfers between devices: 8.95 us -> 8.95 us  [exchange_sum(): lax.ppermute(value, axis, [(at, at ^ step) for at in range(count)])]
where the time goes in v4:
time: 158 us; the launch traced here: 157 us
  waiting for transfers between devices  89.4 us (57%)
  starting transfers between devices  35.4 us (22%)
  Pallas kernels  26.4 us (17%)
  local copies, waits for them, and re-layouts  2.81 us (2%)
    all_to_all x1, waiting for transfers between devices, local(): lax.all_to_all(packed.reshape(frame_count, 4, ROWS, WIDTH), 'seq', split_...  58.9 us
    ppermute x4, waiting for transfers between devices, split_sum(): pieces.append(lax.ppermute(value, ('dp', 'seq'), pairs))  21.5 us
    all_to_all x1, starting transfers between devices, local(): lax.all_to_all(packed.reshape(frame_count, 4, ROWS, WIDTH), 'seq', split_...  11.6 us
    pallas_call x1, Pallas kernels, local(): pl.pallas_call(functools.partial(spatial_kernel, heads), out_shape=[pltpu...  9.22 us
    ppermute x7, waiting for transfers between devices, exchange_sum(): lax.ppermute(value, axis, [(at, at ^ step) for at in range(count)])  8.95 us
    ppermute x7, starting transfers between devices, exchange_sum(): lax.ppermute(value, axis, [(at, at ^ step) for at in range(count)])  8.37 us
    pallas_call x1, Pallas kernels, local(): pl.pallas_call(functools.partial(bias_kernel, frame_count), out_shape=jax...  7.77 us
    all_to_all x1, starting transfers between devices, local(): back = lax.all_to_all(grads, 'seq', split_axis=0, concat_axis=0, tiled=True)  7.5 us
  transfers between devices with their start and end apart: 14, of which 9 were waited for; matrix products, arithmetic and copies ran while one was open for 2% of the time, Pallas kernels for 12%

profile of v4, /device:TPU:4, one launch (start us, length us, event | category | flops | bytes accessed | tf_op | source)
XLA Modules:
  0.0 156.7 jit_solution(9873037837598308258)
XLA Ops:
  0.6 2.8 %pack.1 = bf16[16,2,4,8,1536]{4,3,2,1,0:T(8,128)(2,1)} custom-call(bf16[16,8,6144]{2,1,0:T(8,128)(2,1)} %bitcast.22, bf16[16,8,6144]{2,1,0:T(8,128)(2,1)} %bitcast.24, bf16[16,8,6144]{2,1,0:T(8,128)(2,1)} %bitcast.26, bf16[16,8,6144]{2,1,0:T(8,128)(2,1)} %bitcast.28), custom_call_target="tpu_custom_call" | custom-call | tf_op jit(solution)/shard_map/pack/pallas_call | solution.py:254
  3.5 11.6 %all-to-all-start = ((bf16[32,4,8,1536]{3,2,1,0:T(8,128)(2,1)}), bf16[32,4,8,1536]{3,2,1,0:T(8,128)(2,1)S(1)}, u32[]{:S(2)}, u32[]{:S(2)}) async-start(bf16[32,4,8,1536]{3,2,1,0:T(8,128)(2,1)} %bitcast.21), calls=%async_computation | async-start | bytes 6291456 | tf_op jit(solution)/shard_map/all_to_all | solution.py:267
  15.5 0.2 broadcast_in_dim.36
  15.7 0.8 broadcast_in_dim.37
  16.6 0.2 broadcast_in_dim.34
  16.8 0.6 dynamic_slice.7.length
  18.0 9.2 %spatial.1 = (bf16[128,6144]{1,0:T(8,128)(2,1)}, bf16[128,6144]{1,0:T(8,128)(2,1)}, bf16[128,6144]{1,0:T(8,128)(2,1)}) custom-call(s32[1]{0:T(128)S(6)} %convert_element_type.3.live, bf16[128,6144]{1,0:T(8,128)(2,1)} %bitcast.23, bf16[128,6144]{1,0:T(8,128)(2,1)} %bitcast.25, bf16[128,6144]{1,0:T(8,128)(2,1)} %bitcast.27, bf16[128,6144]{1,0:T(8,128)(2,1)} %bitcast.29), custom_call_target="tpu_custom_call" | custom-call | flops 503316480 | bytes 5505024 | tf_op jit(solution)/shard_map/spatial/pallas_call | solution.py:273
  27.3 58.9 %all-to-all-done.tensors = bf16[32,4,8,1536]{3,2,1,0:T(8,128)(2,1)S(1)} async-done(((bf16[32,4,8,1536]{3,2,1,0:T(8,128)(2,1)}), bf16[32,4,8,1536]{3,2,1,0:T(8,128)(2,1)S(1)}, u32[]{:S(2)}, u32[]{:S(2)}) %all-to-all-start) | async-done | bytes 3145760 | tf_op jit(solution)/shard_map/all_to_all | solution.py:267
  86.2 5.1 %temporal.1 = (bf16[32,3,8,1536]{3,2,1,0:T(8,128)(2,1)}, f32[12,256,256]{2,1,0:T(8,128)}) custom-call(s32[1]{0:T(128)} %dynamic_slice.7.length, bf16[32,4,8,1536]{3,2,1,0:T(8,128)(2,1)S(1)} %all-to-all-done.tensors, f32[12,8,512]{2,1,0:T(8,128)S(1)} %broadcast_select_fusion.seed), custom_call_target="tpu_custom_call" | custom-call | flops 1006632960 | bytes 5505024 | tf_op jit(solution)/shard_map/temporal/pallas_call | solution.py:306
  91.3 7.5 %all-to-all-start.1 = ((bf16[32,3,8,1536]{3,2,1,0:T(8,128)(2,1)}), bf16[32,3,8,1536]{3,2,1,0:T(8,128)(2,1)S(1)}, u32[]{:S(2)}, u32[]{:S(2)}) async-start(bf16[32,3,8,1536]{3,2,1,0:T(8,128)(2,1)} %get-tuple-element.24), calls=%async_computation.1 | async-start | bytes 4718592 | tf_op jit(solution)/shard_map/all_to_all | solution.py:342
  98.9 7.8 %offsets.1 = f32[12,8,512]{2,1,0:T(8,128)S(1)} custom-call(f32[12,256,256]{2,1,0:T(8,128)} %get-tuple-element.31.terms), custom_call_target="tpu_custom_call" | custom-call | flops 3145728 | bytes 3145728 | tf_op jit(solution)/shard_map/offsets/pallas_call | solution.py:327
  106.7 0.2 reduce_sum.14
  106.9 0.2 reduce_sum.18
  107.7 1.2 collective-permute-done
  109.0 1.7 %collective-permute-start.1 = (f32[24,63]{1,0:T(8,128)S(1)}, f32[24,63]{1,0:T(8,128)S(1)}, u32[]{:S(2)}, u32[]{:S(2)}) collective-permute-start(f32[24,63]{1,0:T(8,128)S(1)} %add.49), channel_id=1, source_target_pairs={{0,64},{32,96},{64,0},{96,32},{128,192},{160,224},{192,128},{224,1... | collective-permute-start | bytes 18152 | tf_op jit(solution)/shard_map/ppermute | solution.py:226
  110.7 2.9 %collective-permute-start.2 = (f32[24,63]{1,0:T(8,128)S(1)}, f32[24,63]{1,0:T(8,128)S(1)}, u32[]{:S(2)}, u32[]{:S(2)}) collective-permute-start(f32[24,63]{1,0:T(8,128)S(1)} %add.49), channel_id=1, source_target_pairs={{0,128},{32,160},{64,192},{96,224},{128,0},{160,32},{192,64},{224,... | collective-permute-start | bytes 18152 | tf_op jit(solution)/shard_map/ppermute | solution.py:226
  113.6 0.2 collective-permute-start.3
  113.8 2.1 %collective-permute-done.2 = f32[24,63]{1,0:T(8,128)S(1)} collective-permute-done((f32[24,63]{1,0:T(8,128)S(1)}, f32[24,63]{1,0:T(8,128)S(1)}, u32[]{:S(2)}, u32[]{:S(2)}) %collective-permute-start.2) | collective-permute-done | bytes 6080 | tf_op jit(solution)/shard_map/ppermute | solution.py:226
  115.9 2.6 %collective-permute-done.3 = f32[24,63]{1,0:T(8,128)S(1)} collective-permute-done((f32[24,63]{1,0:T(8,128)S(1)}, f32[24,63]{1,0:T(8,128)S(1)}, u32[]{:S(2)}, u32[]{:S(2)}) %collective-permute-start.3) | collective-permute-done | bytes 6080 | tf_op jit(solution)/shard_map/ppermute | solution.py:226
  118.5 1.1 collective-permute-start.4
  119.6 0.9 collective-permute-start.5
  120.5 1.5 collective-permute-start.6
  122.0 0.2 collective-permute-done.4
  122.2 2.9 %collective-permute-done.5 = f32[24,63]{1,0:T(8,128)S(1)} collective-permute-done((f32[24,63]{1,0:T(8,128)S(1)}, f32[24,63]{1,0:T(8,128)S(1)}, u32[]{:S(2)}, u32[]{:S(2)}) %collective-permute-start.5) | collective-permute-done | bytes 6080 | tf_op jit(solution)/shard_map/ppermute | solution.py:226
  125.1 3.2 %collective-permute-start.10 = (f32[24,63]{1,0:T(8,128)S(1)}, f32[24,63]{1,0:T(8,128)S(1)}, u32[]{:S(2)}, u32[]{:S(2)}) collective-permute-start(f32[24,63]{1,0:T(8,128)S(1)} %add_add_fusion.1), channel_id=1, source_target_pairs={{0,12},{1,13},{2,14},{3,15},{4,8},{5,9},{6,10},{7,11},{8,4},{9,5},... | collective-permute-start | bytes 18152 | tf_op jit(solution)/shard_map/ppermute | solution.py:239
  128.3 0.7 collective-permute-start.7
  129.1 1.2 collective-permute-start.9
  130.3 20.2 %collective-permute-done.10 = f32[24,63]{1,0:T(8,128)S(1)} collective-permute-done((f32[24,63]{1,0:T(8,128)S(1)}, f32[24,63]{1,0:T(8,128)S(1)}, u32[]{:S(2)}, u32[]{:S(2)}) %collective-permute-start.10) | collective-permute-done | bytes 6080 | tf_op jit(solution)/shard_map/ppermute | solution.py:239
  150.5 1.3 collective-permute-done.8
  151.8 2.7 %collective-permute-start.11 = (f32[24,63]{1,0:T(8,128)S(1)}, f32[24,63]{1,0:T(8,128)S(1)}, u32[]{:S(2)}, u32[]{:S(2)}) collective-permute-start(f32[24,63]{1,0:T(8,128)S(1)} %add_add_fusion), channel_id=1, source_target_pairs={{0,32},{32,0},{64,96},{96,64},{128,160},{160,128},{192,224},{224,1... | collective-permute-start | bytes 18152 | tf_op jit(solution)/shard_map/ppermute | solution.py:354
  154.6 1.4 unpack.1
  156.1 0.6 add.59
  (35 shorter events, 1.4 us)
Async XLA Ops:
  3.5 11.7 %copy-start.1 = (f32[24,63]{1,0:T(8,128)S(1)}, f32[24,63]{1,0:T(8,128)}, u32[]{:S(2)}) copy-start(f32[24,63]{1,0:T(8,128)} %param.11) | copy-start | bytes 18148
  3.5 13.3 %copy-start.2 = (s32[8]{0:T(128)S(1)}, s32[8]{0:T(128)}, u32[]{:S(2)}) copy-start(s32[8]{0:T(128)} %param.10) | copy-start | bytes 100
  3.5 82.7 %all-to-all-start = ((bf16[32,4,8,1536]{3,2,1,0:T(8,128)(2,1)}), bf16[32,4,8,1536]{3,2,1,0:T(8,128)(2,1)S(1)}, u32[]{:S(2)}, u32[]{:S(2)}) async-start(bf16[32,4,8,1536]{3,2,1,0:T(8,128)(2,1)} %bitcast.21), calls=%async_computation | async-start | bytes 6291456 | tf_op jit(solution)/shard_map/all_to_all | solution.py:267
  18.0 9.2 %copy-start = (f32[12,512]{1,0:T(8,128)S(1)}, f32[12,512]{1,0:T(8,128)}, u32[]{:S(2)}) copy-start(f32[12,512]{1,0:T(8,128)} %broadcast_in_dim.37) | copy-start | bytes 73732
  91.3 63.3 %all-to-all-start.1 = ((bf16[32,3,8,1536]{3,2,1,0:T(8,128)(2,1)}), bf16[32,3,8,1536]{3,2,1,0:T(8,128)(2,1)S(1)}, u32[]{:S(2)}, u32[]{:S(2)}) async-start(bf16[32,3,8,1536]{3,2,1,0:T(8,128)(2,1)} %get-tuple-element.24), calls=%async_computation.1 | async-start | bytes 4718592 | tf_op jit(solution)/shard_map/all_to_all | solution.py:342
  107.5 1.3 collective-permute-start
  109.0 4.8 %collective-permute-start.1 = (f32[24,63]{1,0:T(8,128)S(1)}, f32[24,63]{1,0:T(8,128)S(1)}, u32[]{:S(2)}, u32[]{:S(2)}) collective-permute-start(f32[24,63]{1,0:T(8,128)S(1)} %add.49), channel_id=1, source_target_pairs={{0,64},{32,96},{64,0},{96,32},{128,192},{160,224},{192,128},{224,1... | collective-permute-start | bytes 18152 | tf_op jit(solution)/shard_map/ppermute | solution.py:226
  110.7 5.2 %collective-permute-start.2 = (f32[24,63]{1,0:T(8,128)S(1)}, f32[24,63]{1,0:T(8,128)S(1)}, u32[]{:S(2)}, u32[]{:S(2)}) collective-permute-start(f32[24,63]{1,0:T(8,128)S(1)} %add.49), channel_id=1, source_target_pairs={{0,128},{32,160},{64,192},{96,224},{128,0},{160,32},{192,64},{224,... | collective-permute-start | bytes 18152 | tf_op jit(solution)/shard_map/ppermute | solution.py:226
  113.6 4.9 %collective-permute-start.3 = (f32[24,63]{1,0:T(8,128)S(1)}, f32[24,63]{1,0:T(8,128)S(1)}, u32[]{:S(2)}, u32[]{:S(2)}) collective-permute-start(f32[24,63]{1,0:T(8,128)S(1)} %add.49), channel_id=1, source_target_pairs={{0,192},{32,224},{64,128},{96,160},{128,64},{160,96},{192,0},{224,... | collective-permute-start | bytes 18152 | tf_op jit(solution)/shard_map/ppermute | solution.py:226
  118.5 3.7 %collective-permute-start.4 = (f32[24,63]{1,0:T(8,128)S(1)}, f32[24,63]{1,0:T(8,128)S(1)}, u32[]{:S(2)}, u32[]{:S(2)}) collective-permute-start(f32[24,63]{1,0:T(8,128)S(1)} %add_add_fusion.2), channel_id=1, source_target_pairs={{0,1},{1,0},{2,3},{3,2},{4,5},{5,4},{6,7},{7,6},{8,9},{9,8},{10,11... | collective-permute-start | bytes 18152 | tf_op jit(solution)/shard_map/ppermute | solution.py:226
  119.6 5.4 %collective-permute-start.5 = (f32[24,63]{1,0:T(8,128)S(1)}, f32[24,63]{1,0:T(8,128)S(1)}, u32[]{:S(2)}, u32[]{:S(2)}) collective-permute-start(f32[24,63]{1,0:T(8,128)S(1)} %add_add_fusion.2), channel_id=1, source_target_pairs={{0,2},{1,3},{2,0},{3,1},{4,6},{5,7},{6,4},{7,5},{8,10},{9,11},{10,... | collective-permute-start | bytes 18152 | tf_op jit(solution)/shard_map/ppermute | solution.py:226
  120.5 4.6 %collective-permute-start.6 = (f32[24,63]{1,0:T(8,128)S(1)}, f32[24,63]{1,0:T(8,128)S(1)}, u32[]{:S(2)}, u32[]{:S(2)}) collective-permute-start(f32[24,63]{1,0:T(8,128)S(1)} %add_add_fusion.2), channel_id=1, source_target_pairs={{0,3},{1,2},{2,1},{3,0},{4,7},{5,6},{6,5},{7,4},{8,11},{9,10},{10,... | collective-permute-start | bytes 18152 | tf_op jit(solution)/shard_map/ppermute | solution.py:226
  125.1 25.5 %collective-permute-start.10 = (f32[24,63]{1,0:T(8,128)S(1)}, f32[24,63]{1,0:T(8,128)S(1)}, u32[]{:S(2)}, u32[]{:S(2)}) collective-permute-start(f32[24,63]{1,0:T(8,128)S(1)} %add_add_fusion.1), channel_id=1, source_target_pairs={{0,12},{1,13},{2,14},{3,15},{4,8},{5,9},{6,10},{7,11},{8,4},{9,5},... | collective-permute-start | bytes 18152 | tf_op jit(solution)/shard_map/ppermute | solution.py:239
  128.3 22.2 %collective-permute-start.7 = (f32[24,63]{1,0:T(8,128)S(1)}, f32[24,63]{1,0:T(8,128)S(1)}, u32[]{:S(2)}, u32[]{:S(2)}) collective-permute-start(f32[24,63]{1,0:T(8,128)S(1)} %add_add_fusion.1), channel_id=1, source_target_pairs={{0,0},{1,1},{2,2},{3,3},{4,4},{5,5},{6,6},{7,7},{8,8},{9,9},{10,10... | collective-permute-start | bytes 18152 | tf_op jit(solution)/shard_map/ppermute | solution.py:239
  129.0 22.8 %collective-permute-start.8 = (f32[24,63]{1,0:T(8,128)S(1)}, f32[24,63]{1,0:T(8,128)S(1)}, u32[]{:S(2)}, u32[]{:S(2)}) collective-permute-start(f32[24,63]{1,0:T(8,128)S(1)} %add_add_fusion.1), channel_id=1, source_target_pairs={{0,4},{1,5},{2,6},{3,7},{4,0},{5,1},{6,2},{7,3},{8,12},{9,13},{10,... | collective-permute-start | bytes 18152 | tf_op jit(solution)/shard_map/ppermute | solution.py:239
  129.1 22.7 %collective-permute-start.9 = (f32[24,63]{1,0:T(8,128)S(1)}, f32[24,63]{1,0:T(8,128)S(1)}, u32[]{:S(2)}, u32[]{:S(2)}) collective-permute-start(f32[24,63]{1,0:T(8,128)S(1)} %add_add_fusion.1), channel_id=1, source_target_pairs={{0,8},{1,9},{2,10},{3,11},{4,12},{5,13},{6,14},{7,15},{8,0},{9,1},... | collective-permute-start | bytes 18152 | tf_op jit(solution)/shard_map/ppermute | solution.py:239
  151.8 4.3 %collective-permute-start.11 = (f32[24,63]{1,0:T(8,128)S(1)}, f32[24,63]{1,0:T(8,128)S(1)}, u32[]{:S(2)}, u32[]{:S(2)}) collective-permute-start(f32[24,63]{1,0:T(8,128)S(1)} %add_add_fusion), channel_id=1, source_target_pairs={{0,32},{32,0},{64,96},{96,64},{128,160},{160,128},{192,224},{224,1... | collective-permute-start | bytes 18152 | tf_op jit(solution)/shard_map/ppermute | solution.py:354

commit v5 on v4

--- a/solution.py
+++ b/solution.py
@@ -96,18 +96,22 @@
         copy.wait()
 
 
-def spatial_kernel(heads, live, query, keys, values, grad, grad_query, grad_keys, grad_values):
-    flag = live[0].astype(WIDE).astype(LOW)
-    for head in range(heads):
-        cols = pl.ds(head * HDIM, HDIM)
-        tokens = query[:, cols], keys[:, cols], values[:, cols], grad[:, cols] * flag
-        attention_low, grad_logits = soften(*products(*tokens), None)
-        outs = token_grads(
-            attention_low, grad_logits.astype(LOW), tokens[0], tokens[1], tokens[3]
-        )
-        grad_query[:, cols] = outs[0]
-        grad_keys[:, cols] = outs[1]
-        grad_values[:, cols] = outs[2]
+def spatial_kernel(heads, core, frames, place_here, query, keys, values, grad, *outputs):
+    grad_query, grad_keys, grad_values = outputs[-3:]
+
+    @pl.when(place_here[0] % 2 == core)
+    def _():
+        flag = jnp.where(place_here[1] < frames[place_here[0]], 1.0, 0.0).astype(LOW)
+        for head in range(heads):
+            cols = pl.ds(head * HDIM, HDIM)
+            tokens = query[:, cols], keys[:, cols], values[:, cols], grad[:, cols] * flag
+            attention_low, grad_logits = soften(*products(*tokens), None)
+            outs = token_grads(
+                attention_low, grad_logits.astype(LOW), tokens[0], tokens[1], tokens[3]
+            )
+            grad_query[:, cols] = outs[0]
+            grad_keys[:, cols] = outs[1]
+            grad_values[:, cols] = outs[2]
 
 
 def moved_rows(seed, frame_count, length):
@@ -244,7 +248,6 @@
     frame_count = lax.axis_size("seq")
     frame_index = lax.axis_index("seq")
     length = lax.dynamic_index_in_dim(frames, lax.axis_index("dp"), 0, keepdims=True)
-    live = (frame_index < length).astype(jnp.int32)
     patches, columns = query.shape[2], query.shape[3]
     groups = patches // ROWS
     tokens = frame_count * ROWS
@@ -264,29 +267,44 @@
         compiler_params=params(8),
         name="pack",
     )(*place(pltpu.HBM, *tiled))
+    heads = 4
+    blocks = SHEADS // heads
+    place_here = jnp.stack([lax.axis_index("dp"), frame_index]).astype(jnp.int32)
+
+    def spatial_part(core, earlier):
+        block = pl.BlockSpec(
+            (patches, heads * HDIM),
+            lambda at, frames, here: (0, jnp.where(here[0] % 2 == core, at, blocks)),
+        )
+        return pl.pallas_call(
+            functools.partial(spatial_kernel, heads, core),
+            out_shape=[pltpu.HBM((patches, columns), LOW)] * 3,
+            grid_spec=pltpu.PrefetchScalarGridSpec(
+                num_scalar_prefetch=2,
+                grid=(blocks,),
+                in_specs=[block] * 4 + [spec(pl.ANY)] * len(earlier),
+                out_specs=[block] * 3,
+            ),
+            input_output_aliases={6 + number: number for number in range(len(earlier))},
+            compiler_params=params(16),
+            cost_estimate=pl.CostEstimate(
+                flops=10 * SHEADS * patches * patches * HDIM,
+                bytes_accessed=14 * patches * SPATIAL,
+                transcendentals=SHEADS * patches * patches,
+            ),
+            name="spatial",
+        )(
+            frames,
+            place_here,
+            *place(pltpu.HBM, *flat, *earlier),
+        )
+
+    spatial = spatial_part(0, ())
+    packed, *spatial = lax.optimization_barrier((packed, *spatial))
     gathered = lax.all_to_all(
         packed.reshape(frame_count, 4, ROWS, WIDTH), "seq", split_axis=0, concat_axis=0, tiled=True
     )
-
-    heads = 4
-    block = pl.BlockSpec((patches, heads * HDIM), lambda at, live: (0, at))
-    spatial = pl.pallas_call(
-        functools.partial(spatial_kernel, heads),
-        out_shape=[pltpu.HBM((patches, columns), LOW)] * 3,
-        grid_spec=pltpu.PrefetchScalarGridSpec(
-            num_scalar_prefetch=1,
-            grid=(SHEADS // heads,),
-            in_specs=[block] * 4,
-            out_specs=[block] * 3,
-        ),
-        compiler_params=params(16),
-        cost_estimate=pl.CostEstimate(
-            flops=10 * SHEADS * patches * patches * HDIM,
-            bytes_accessed=14 * patches * SPATIAL,
-            transcendentals=SHEADS * patches * patches,
-        ),
-        name="spatial",
-    )(live, *place(pltpu.HBM, *flat))
+    spatial = spatial_part(1, spatial)
 
     half = frame_index % HALVES
     bias_here = lax.dynamic_slice_in_dim(bias, half * HEADS_HERE, HEADS_HERE, 0)

time: 158 us -> 155 us (0.981)
  starting transfers between devices: 35.4 us -> 30.8 us
  Pallas kernels: 26.4 us -> 29.9 us
    ppermute x4, waiting for transfers between devices: 21.5 us -> 15.5 us  [split_sum(): pieces.append(lax.ppermute(value, ('dp', 'seq'), pairs))]
    pallas_call x1 -> x2, Pallas kernels: 9.22 us -> 12.6 us  [spatial_part(): pl.pallas_call(functools.partial(spatial_kernel, heads, core), out_shape=...]
    ppermute x1, starting transfers between devices: 2.71 us -> 0.09 us  [local(): lax.ppermute(sums, 'dp', [(clip, clip ^ 1) for clip in range(lax.axis_siz...]
    all_to_all x1, waiting for transfers between devices: 0.08 us -> 2.49 us  [local(): back = lax.all_to_all(grads, 'seq', split_axis=0, concat_axis=0, tiled=True)]
    all_to_all x1, starting transfers between devices: 7.5 us -> 5.44 us  [local(): back = lax.all_to_all(grads, 'seq', split_axis=0, concat_axis=0, tiled=True)]
    all_to_all x1, waiting for transfers between devices: 58.9 us -> 60.7 us  [local(): lax.all_to_all(packed.reshape(frame_count, 4, ROWS, WIDTH), 'seq', split_...]
  transfers between devices with their start and end apart: 14 -> 14, of which waited for: 9 -> 9; matrix products, arithmetic and copies ran while one was open for 2% -> 2% of each run, Pallas kernels for 12% -> 8%
where the time goes in v5:
time: 155 us; the launch traced here: 154 us
  waiting for transfers between devices  88.3 us (57%)
  starting transfers between devices  30.8 us (20%)
  Pallas kernels  29.9 us (19%)
  local copies, waits for them, and re-layouts  2.81 us (2%)
    all_to_all x1, waiting for transfers between devices, local(): lax.all_to_all(packed.reshape(frame_count, 4, ROWS, WIDTH), 'seq', split_...  60.7 us
    ppermute x4, waiting for transfers between devices, split_sum(): pieces.append(lax.ppermute(value, ('dp', 'seq'), pairs))  15.5 us
    pallas_call x2, Pallas kernels, spatial_part(): pl.pallas_call(functools.partial(spatial_kernel, heads, core), out_shape=...  12.6 us
    all_to_all x1, starting transfers between devices, local(): lax.all_to_all(packed.reshape(frame_count, 4, ROWS, WIDTH), 'seq', split_...  11.7 us
    ppermute x7, waiting for transfers between devices, exchange_sum(): lax.ppermute(value, axis, [(at, at ^ step) for at in range(count)])  9.61 us
    ppermute x7, starting transfers between devices, exchange_sum(): lax.ppermute(value, axis, [(at, at ^ step) for at in range(count)])  8.37 us
    pallas_call x1, Pallas kernels, local(): pl.pallas_call(functools.partial(bias_kernel, frame_count), out_shape=jax...  7.77 us
    all_to_all x1, starting transfers between devices, local(): back = lax.all_to_all(grads, 'seq', split_axis=0, concat_axis=0, tiled=True)  5.44 us
  transfers between devices with their start and end apart: 14, of which 9 were waited for; matrix products, arithmetic and copies ran while one was open for 2% of the time, Pallas kernels for 8%

profile of v5, /device:TPU:4, one launch (start us, length us, event | category | flops | bytes accessed | tf_op | source)
XLA Modules:
  0.0 153.8 jit_solution(7950105212812018087)
XLA Ops:
  0.7 2.8 %pack.1 = bf16[16,2,4,8,1536]{4,3,2,1,0:T(8,128)(2,1)} custom-call(bf16[16,8,6144]{2,1,0:T(8,128)(2,1)} %bitcast.22, bf16[16,8,6144]{2,1,0:T(8,128)(2,1)} %bitcast.25, bf16[16,8,6144]{2,1,0:T(8,128)(2,1)} %bitcast.28, bf16[16,8,6144]{2,1,0:T(8,128)(2,1)} %bitcast.31), custom_call_target="tpu_custom_call" | custom-call | tf_op jit(solution)/shard_map/pack/pallas_call | solution.py:257
  3.5 10.2 %spatial.2 = (bf16[128,6144]{1,0:T(8,128)(2,1)}, bf16[128,6144]{1,0:T(8,128)(2,1)}, bf16[128,6144]{1,0:T(8,128)(2,1)}) custom-call(s32[8]{0:T(128)S(1)} %copy-done, s32[2]{0:T(128)S(1)} %pad_add_fusion.place_here, bf16[128,6144]{1,0:T(8,128)(2,1)} %bitcast.23, bf16[128,6144]{1,0:T(8,128)(2,1)} %bitcast.26, bf16[128,6144]{1,0:T(8,128)(2,1)} %bitcast.29, ...), custom_call_target="tpu_custom_call" | custom-call | flops 503316480 | bytes 5505024 | tf_op jit(solution)/shard_map/spatial/pallas_call | solution.py:279
  13.7 11.7 %all-to-all-start = ((bf16[32,4,8,1536]{3,2,1,0:T(8,128)(2,1)}), bf16[32,4,8,1536]{3,2,1,0:T(8,128)(2,1)S(1)}, u32[]{:S(2)}, u32[]{:S(2)}) async-start(bf16[32,4,8,1536]{3,2,1,0:T(8,128)(2,1)} %bitcast.34), calls=%async_computation | async-start | bytes 6291456 | tf_op jit(solution)/shard_map/all_to_all | solution.py:304
  26.0 0.8 broadcast_in_dim.37
  26.9 0.2 broadcast_in_dim.34
  27.1 0.6 dynamic_slice.7.length
  27.7 2.4 %spatial.3 = (bf16[128,6144]{1,0:T(8,128)(2,1)}, bf16[128,6144]{1,0:T(8,128)(2,1)}, bf16[128,6144]{1,0:T(8,128)(2,1)}) custom-call(s32[8]{0:T(128)S(1)} %copy-done, s32[2]{0:T(128)S(1)} %pad_add_fusion.place_here, bf16[128,6144]{1,0:T(8,128)(2,1)} %bitcast.24, ...), custom_call_target="tpu_custom_call", output_to_operand_aliasing={{0}: (6, {}), {1}: (7, {}), {2}: (8, {})} | custom-call | flops 503316480 | bytes 5505024 | tf_op jit(solution)/shard_map/spatial/pallas_call | solution.py:279
  30.1 60.7 %all-to-all-done.tensors = bf16[32,4,8,1536]{3,2,1,0:T(8,128)(2,1)S(1)} async-done(((bf16[32,4,8,1536]{3,2,1,0:T(8,128)(2,1)}), bf16[32,4,8,1536]{3,2,1,0:T(8,128)(2,1)S(1)}, u32[]{:S(2)}, u32[]{:S(2)}) %all-to-all-start) | async-done | bytes 3145760 | tf_op jit(solution)/shard_map/all_to_all | solution.py:304
  90.8 5.3 %temporal.1 = (bf16[32,3,8,1536]{3,2,1,0:T(8,128)(2,1)}, f32[12,256,256]{2,1,0:T(8,128)}) custom-call(s32[1]{0:T(128)} %dynamic_slice.7.length, bf16[32,4,8,1536]{3,2,1,0:T(8,128)(2,1)S(1)} %all-to-all-done.tensors, f32[12,8,512]{2,1,0:T(8,128)S(1)} %broadcast_select_fusion.seed), custom_call_target="tpu_custom_call" | custom-call | flops 1006632960 | bytes 5505024 | tf_op jit(solution)/shard_map/temporal/pallas_call | solution.py:324
  96.1 5.4 %all-to-all-start.1 = ((bf16[32,3,8,1536]{3,2,1,0:T(8,128)(2,1)}), bf16[32,3,8,1536]{3,2,1,0:T(8,128)(2,1)S(1)}, u32[]{:S(2)}, u32[]{:S(2)}) async-start(bf16[32,3,8,1536]{3,2,1,0:T(8,128)(2,1)} %get-tuple-element.38), calls=%async_computation.1 | async-start | bytes 4718592 | tf_op jit(solution)/shard_map/all_to_all | solution.py:360
  101.6 7.8 %offsets.1 = f32[12,8,512]{2,1,0:T(8,128)S(1)} custom-call(f32[12,256,256]{2,1,0:T(8,128)} %get-tuple-element.45.terms), custom_call_target="tpu_custom_call" | custom-call | flops 3145728 | bytes 3145728 | tf_op jit(solution)/shard_map/offsets/pallas_call | solution.py:345
  109.4 0.2 reduce_sum.14
  109.6 0.2 reduce_sum.18
  110.4 1.2 collective-permute-done
  111.7 1.7 %collective-permute-start.1 = (f32[24,63]{1,0:T(8,128)S(1)}, f32[24,63]{1,0:T(8,128)S(1)}, u32[]{:S(2)}, u32[]{:S(2)}) collective-permute-start(f32[24,63]{1,0:T(8,128)S(1)} %add.49), channel_id=1, source_target_pairs={{0,64},{32,96},{64,0},{96,32},{128,192},{160,224},{192,128},{224,1... | collective-permute-start | bytes 18152 | tf_op jit(solution)/shard_map/ppermute | solution.py:230
  113.4 2.9 %collective-permute-start.2 = (f32[24,63]{1,0:T(8,128)S(1)}, f32[24,63]{1,0:T(8,128)S(1)}, u32[]{:S(2)}, u32[]{:S(2)}) collective-permute-start(f32[24,63]{1,0:T(8,128)S(1)} %add.49), channel_id=1, source_target_pairs={{0,128},{32,160},{64,192},{96,224},{128,0},{160,32},{192,64},{224,... | collective-permute-start | bytes 18152 | tf_op jit(solution)/shard_map/ppermute | solution.py:230
  116.3 0.2 collective-permute-start.3
  116.5 2.1 %collective-permute-done.2 = f32[24,63]{1,0:T(8,128)S(1)} collective-permute-done((f32[24,63]{1,0:T(8,128)S(1)}, f32[24,63]{1,0:T(8,128)S(1)}, u32[]{:S(2)}, u32[]{:S(2)}) %collective-permute-start.2) | collective-permute-done | bytes 6080 | tf_op jit(solution)/shard_map/ppermute | solution.py:230
  118.6 2.6 %collective-permute-done.3 = f32[24,63]{1,0:T(8,128)S(1)} collective-permute-done((f32[24,63]{1,0:T(8,128)S(1)}, f32[24,63]{1,0:T(8,128)S(1)}, u32[]{:S(2)}, u32[]{:S(2)}) %collective-permute-start.3) | collective-permute-done | bytes 6080 | tf_op jit(solution)/shard_map/ppermute | solution.py:230
  121.2 1.1 collective-permute-start.4
  122.4 0.9 collective-permute-start.5
  123.2 1.5 collective-permute-start.6
  124.7 0.7 collective-permute-done.4
  125.4 3.1 %collective-permute-done.5 = f32[24,63]{1,0:T(8,128)S(1)} collective-permute-done((f32[24,63]{1,0:T(8,128)S(1)}, f32[24,63]{1,0:T(8,128)S(1)}, u32[]{:S(2)}, u32[]{:S(2)}) %collective-permute-start.5) | collective-permute-done | bytes 6080 | tf_op jit(solution)/shard_map/ppermute | solution.py:230
  128.5 2.6 %collective-permute-start.10 = (f32[24,63]{1,0:T(8,128)S(1)}, f32[24,63]{1,0:T(8,128)S(1)}, u32[]{:S(2)}, u32[]{:S(2)}) collective-permute-start(f32[24,63]{1,0:T(8,128)S(1)} %add_add_fusion.1), channel_id=1, source_target_pairs={{0,12},{1,13},{2,14},{3,15},{4,8},{5,9},{6,10},{7,11},{8,4},{9,5},... | collective-permute-start | bytes 18152 | tf_op jit(solution)/shard_map/ppermute | solution.py:243
  131.1 0.7 collective-permute-start.7
  131.9 1.8 %collective-permute-start.9 = (f32[24,63]{1,0:T(8,128)S(1)}, f32[24,63]{1,0:T(8,128)S(1)}, u32[]{:S(2)}, u32[]{:S(2)}) collective-permute-start(f32[24,63]{1,0:T(8,128)S(1)} %add_add_fusion.1), channel_id=1, source_target_pairs={{0,8},{1,9},{2,10},{3,11},{4,12},{5,13},{6,14},{7,15},{8,0},{9,1},... | collective-permute-start | bytes 18152 | tf_op jit(solution)/shard_map/ppermute | solution.py:243
  133.7 14.2 %collective-permute-done.10 = f32[24,63]{1,0:T(8,128)S(1)} collective-permute-done((f32[24,63]{1,0:T(8,128)S(1)}, f32[24,63]{1,0:T(8,128)S(1)}, u32[]{:S(2)}, u32[]{:S(2)}) %collective-permute-start.10) | collective-permute-done | bytes 6080 | tf_op jit(solution)/shard_map/ppermute | solution.py:243
  147.9 1.3 collective-permute-done.8
  149.3 2.5 %all-to-all-done.1 = bf16[32,3,8,1536]{3,2,1,0:T(8,128)(2,1)S(1)} async-done(((bf16[32,3,8,1536]{3,2,1,0:T(8,128)(2,1)}), bf16[32,3,8,1536]{3,2,1,0:T(8,128)(2,1)S(1)}, u32[]{:S(2)}, u32[]{:S(2)}) %all-to-all-start.1) | async-done | bytes 2359328 | tf_op jit(solution)/shard_map/all_to_all | solution.py:360
  151.8 1.4 unpack.1
  153.2 0.6 add.59
  (37 shorter events, 1.7 us)
Async XLA Ops:
  0.7 2.8 %copy-start = (s32[8]{0:T(128)S(1)}, s32[8]{0:T(128)}, u32[]{:S(2)}) copy-start(s32[8]{0:T(128)} %frames.3) | copy-start | bytes 100
  13.7 11.7 %copy-start.2 = (f32[24,63]{1,0:T(8,128)S(1)}, f32[24,63]{1,0:T(8,128)}, u32[]{:S(2)}) copy-start(f32[24,63]{1,0:T(8,128)} %param.11) | copy-start | bytes 18148
  13.7 77.1 %all-to-all-start = ((bf16[32,4,8,1536]{3,2,1,0:T(8,128)(2,1)}), bf16[32,4,8,1536]{3,2,1,0:T(8,128)(2,1)S(1)}, u32[]{:S(2)}, u32[]{:S(2)}) async-start(bf16[32,4,8,1536]{3,2,1,0:T(8,128)(2,1)} %bitcast.34), calls=%async_computation | async-start | bytes 6291456 | tf_op jit(solution)/shard_map/all_to_all | solution.py:304
  27.7 2.4 %copy-start.1 = (f32[12,512]{1,0:T(8,128)S(1)}, f32[12,512]{1,0:T(8,128)}, u32[]{:S(2)}) copy-start(f32[12,512]{1,0:T(8,128)} %broadcast_in_dim.37) | copy-start | bytes 73732
  96.1 55.6 %all-to-all-start.1 = ((bf16[32,3,8,1536]{3,2,1,0:T(8,128)(2,1)}), bf16[32,3,8,1536]{3,2,1,0:T(8,128)(2,1)S(1)}, u32[]{:S(2)}, u32[]{:S(2)}) async-start(bf16[32,3,8,1536]{3,2,1,0:T(8,128)(2,1)} %get-tuple-element.38), calls=%async_computation.1 | async-start | bytes 4718592 | tf_op jit(solution)/shard_map/all_to_all | solution.py:360
  110.3 1.3 collective-permute-start
  111.7 4.8 %collective-permute-start.1 = (f32[24,63]{1,0:T(8,128)S(1)}, f32[24,63]{1,0:T(8,128)S(1)}, u32[]{:S(2)}, u32[]{:S(2)}) collective-permute-start(f32[24,63]{1,0:T(8,128)S(1)} %add.49), channel_id=1, source_target_pairs={{0,64},{32,96},{64,0},{96,32},{128,192},{160,224},{192,128},{224,1... | collective-permute-start | bytes 18152 | tf_op jit(solution)/shard_map/ppermute | solution.py:230
  113.4 5.2 %collective-permute-start.2 = (f32[24,63]{1,0:T(8,128)S(1)}, f32[24,63]{1,0:T(8,128)S(1)}, u32[]{:S(2)}, u32[]{:S(2)}) collective-permute-start(f32[24,63]{1,0:T(8,128)S(1)} %add.49), channel_id=1, source_target_pairs={{0,128},{32,160},{64,192},{96,224},{128,0},{160,32},{192,64},{224,... | collective-permute-start | bytes 18152 | tf_op jit(solution)/shard_map/ppermute | solution.py:230
  116.3 4.9 %collective-permute-start.3 = (f32[24,63]{1,0:T(8,128)S(1)}, f32[24,63]{1,0:T(8,128)S(1)}, u32[]{:S(2)}, u32[]{:S(2)}) collective-permute-start(f32[24,63]{1,0:T(8,128)S(1)} %add.49), channel_id=1, source_target_pairs={{0,192},{32,224},{64,128},{96,160},{128,64},{160,96},{192,0},{224,... | collective-permute-start | bytes 18152 | tf_op jit(solution)/shard_map/ppermute | solution.py:230
  121.2 4.2 %collective-permute-start.4 = (f32[24,63]{1,0:T(8,128)S(1)}, f32[24,63]{1,0:T(8,128)S(1)}, u32[]{:S(2)}, u32[]{:S(2)}) collective-permute-start(f32[24,63]{1,0:T(8,128)S(1)} %add_add_fusion.2), channel_id=1, source_target_pairs={{0,1},{1,0},{2,3},{3,2},{4,5},{5,4},{6,7},{7,6},{8,9},{9,8},{10,11... | collective-permute-start | bytes 18152 | tf_op jit(solution)/shard_map/ppermute | solution.py:230
  122.4 6.1 %collective-permute-start.5 = (f32[24,63]{1,0:T(8,128)S(1)}, f32[24,63]{1,0:T(8,128)S(1)}, u32[]{:S(2)}, u32[]{:S(2)}) collective-permute-start(f32[24,63]{1,0:T(8,128)S(1)} %add_add_fusion.2), channel_id=1, source_target_pairs={{0,2},{1,3},{2,0},{3,1},{4,6},{5,7},{6,4},{7,5},{8,10},{9,11},{10,... | collective-permute-start | bytes 18152 | tf_op jit(solution)/shard_map/ppermute | solution.py:230
  123.2 5.2 %collective-permute-start.6 = (f32[24,63]{1,0:T(8,128)S(1)}, f32[24,63]{1,0:T(8,128)S(1)}, u32[]{:S(2)}, u32[]{:S(2)}) collective-permute-start(f32[24,63]{1,0:T(8,128)S(1)} %add_add_fusion.2), channel_id=1, source_target_pairs={{0,3},{1,2},{2,1},{3,0},{4,7},{5,6},{6,5},{7,4},{8,11},{9,10},{10,... | collective-permute-start | bytes 18152 | tf_op jit(solution)/shard_map/ppermute | solution.py:230
  128.5 19.4 %collective-permute-start.10 = (f32[24,63]{1,0:T(8,128)S(1)}, f32[24,63]{1,0:T(8,128)S(1)}, u32[]{:S(2)}, u32[]{:S(2)}) collective-permute-start(f32[24,63]{1,0:T(8,128)S(1)} %add_add_fusion.1), channel_id=1, source_target_pairs={{0,12},{1,13},{2,14},{3,15},{4,8},{5,9},{6,10},{7,11},{8,4},{9,5},... | collective-permute-start | bytes 18152 | tf_op jit(solution)/shard_map/ppermute | solution.py:243
  131.1 16.7 %collective-permute-start.7 = (f32[24,63]{1,0:T(8,128)S(1)}, f32[24,63]{1,0:T(8,128)S(1)}, u32[]{:S(2)}, u32[]{:S(2)}) collective-permute-start(f32[24,63]{1,0:T(8,128)S(1)} %add_add_fusion.1), channel_id=1, source_target_pairs={{0,0},{1,1},{2,2},{3,3},{4,4},{5,5},{6,6},{7,7},{8,8},{9,9},{10,10... | collective-permute-start | bytes 18152 | tf_op jit(solution)/shard_map/ppermute | solution.py:243
  131.8 17.4 %collective-permute-start.8 = (f32[24,63]{1,0:T(8,128)S(1)}, f32[24,63]{1,0:T(8,128)S(1)}, u32[]{:S(2)}, u32[]{:S(2)}) collective-permute-start(f32[24,63]{1,0:T(8,128)S(1)} %add_add_fusion.1), channel_id=1, source_target_pairs={{0,4},{1,5},{2,6},{3,7},{4,0},{5,1},{6,2},{7,3},{8,12},{9,13},{10,... | collective-permute-start | bytes 18152 | tf_op jit(solution)/shard_map/ppermute | solution.py:243
  131.9 17.3 %collective-permute-start.9 = (f32[24,63]{1,0:T(8,128)S(1)}, f32[24,63]{1,0:T(8,128)S(1)}, u32[]{:S(2)}, u32[]{:S(2)}) collective-permute-start(f32[24,63]{1,0:T(8,128)S(1)} %add_add_fusion.1), channel_id=1, source_target_pairs={{0,8},{1,9},{2,10},{3,11},{4,12},{5,13},{6,14},{7,15},{8,0},{9,1},... | collective-permute-start | bytes 18152 | tf_op jit(solution)/shard_map/ppermute | solution.py:243
  149.2 4.0 %collective-permute-start.11 = (f32[24,63]{1,0:T(8,128)S(1)}, f32[24,63]{1,0:T(8,128)S(1)}, u32[]{:S(2)}, u32[]{:S(2)}) collective-permute-start(f32[24,63]{1,0:T(8,128)S(1)} %add_add_fusion), channel_id=1, source_target_pairs={{0,32},{32,0},{64,96},{96,64},{128,160},{160,128},{192,224},{224,1... | collective-permute-start | bytes 18152 | tf_op jit(solution)/shard_map/ppermute | solution.py:372
